TPU v7x, 128 devices: a whole 4x4x4 slice. The times are simulated.
128 devices in a mesh: slab: 16 (over x, z_hi, core), grp: 8 (over y, z_lo).
Axes of the slice: x: 4, y: 4, z: 4 (z_hi: 2, z_lo: 2; z = z_hi * 2 + z_lo), core: 2. Of those that a mesh axis runs over, the one named last changes fastest.
Arguments:
- src_pos: float32 [16, 8, 3, 4096], P('slab', 'grp'), may hold values from 0 to 1
- src_vort: float32 [16, 8, 3, 4096], P('slab', 'grp'), may hold values from -6 to 6
- face_valid: int32 [16, 8, 2, 2048], P('slab', 'grp'), may hold values 0 or 1
- tgt_pos: float32 [16, 8, 3, 128], P('slab', 'grp'), may hold values from 0 to 1
- tgt_vort: float32 [16, 8, 3, 128], P('slab', 'grp'), may hold values from -6 to 6
- mig_pos: float32 [16, 8, 3, 96], P('slab', 'grp'), may hold values from 0 to 1
- mig_vort: float32 [16, 8, 3, 96], P('slab', 'grp'), may hold values from -6 to 6
- mig_valid: int32 [16, 8, 96], P('slab', 'grp'), may hold values 0 or 1
- mig_route: int32 [16, 8, 96, 1], P('slab', 'grp'), may hold values from 0 to 15; in each aligned block of 96 rows (0 to 95, 96 to 191, ..., all dimensions but the last counted through in order) at most 8 rows name the same one
Outputs:
- moved_pos: float32 [16, 8, 3, 256], P('slab', 'grp')
- moved_vort: float32 [16, 8, 3, 256], P('slab', 'grp')
Inputs may be any that keep to these rules, and one draw needn't show every extreme that they name: `mig_route`: value d sends a row to member d mod 8 of the slab below when d < 8, else of the slab above; the rows of one device name one value at most 8 times, and some device reaches 8.
All inputs are finite; a program needn't handle non-finite values. No bound on the sum of `face_valid` or of `mig_valid` on one device may be relied on, other than what follows from the above.
Results may differ from a plain program's by a relative error of at most 0.00065.
Values sent between devices are 32-bit elements; how exact they have to be, the bound alone decides.
No kernel may reach another device: no remote copies, remote signals or barrier semaphores. Data moves between devices by JAX's collectives and lax.ppermute only.
A program may use at most 128 MiB of HBM per device.

v0:
```python
import math

import jax
import jax.numpy as jnp
from jax import lax
from jax.sharding import PartitionSpec as P

CAP = 8
STEPS = 2


core_square = 0.0225
time_step = 0.1
strength = 0.03 / (4.0 * math.pi)
highest = lax.Precision.HIGHEST


def padded_2(cells, sides, width):
    for axis, dim in sides:
        count = lax.axis_size(axis)
        head = lax.slice_in_dim(cells, 0, width, axis=dim)
        tail = lax.slice_in_dim(cells, cells.shape[dim] - width, cells.shape[dim], axis=dim)
        cells = jnp.concatenate(
            [
                lax.ppermute(tail, axis, [(i, (i + 1) % count) for i in range(count)]),
                cells,
                lax.ppermute(head, axis, [((i + 1) % count, i) for i in range(count)]),
            ],
            axis=dim,
        )
    return cells


def expand(places, vortex):
    length = places.shape[1]
    squares = jnp.sum(places * places, axis=0, keepdims=True)
    curled = jnp.cross(places, vortex, axis=0)
    outer_vort = (places[:, None, :] * vortex[None, :, :]).reshape(9, length)
    outer_curl = (places[:, None, :] * curled[None, :, :]).reshape(9, length)
    return jnp.concatenate([places, squares, vortex, curled, outer_vort, outer_curl], axis=0)


def field_sums(where_pos, where_sq, features):
    length = features.shape[1]
    count = where_pos.shape[1]
    widest = 1 << max(9, min(14, (4194304 // count).bit_length() - 1))
    block_width = math.gcd(length, widest)

    def one_block(iteration, running):
        block = lax.dynamic_slice_in_dim(features, iteration * block_width, block_width, 1)
        inner_dot = lax.dot_general(
            block[0:3],
            where_pos,
            (((0,), (0,)), ((), ())),
            precision=highest,
            preferred_element_type=jnp.float32,
        )
        distance = block[3][:, None] + where_sq[None, :] - 2.0 * inner_dot
        inverse = 1.0 / (distance + core_square)
        root_inv = jnp.sqrt(inverse)
        qweight = (distance + 2.5 * core_square) * inverse * inverse * root_inv
        fweight = -(3.0 * distance + 10.5 * core_square) * inverse * inverse * inverse * root_inv
        near_sums = jnp.dot(
            block[4:10], qweight, precision=highest, preferred_element_type=jnp.float32
        )
        grad_sums = jnp.dot(
            block[4:28], fweight, precision=highest, preferred_element_type=jnp.float32
        )
        return running + jnp.concatenate([near_sums, grad_sums], axis=0)

    start = jnp.zeros((30, count), jnp.float32)
    return lax.fori_loop(0, length // block_width, one_block, start)


def rates_from(where_pos, where_vort, blocks):
    where_sq = jnp.sum(where_pos * where_pos, axis=0)
    joined = blocks[0]
    sums = field_sums(where_pos, where_sq, joined)
    count = where_pos.shape[1]
    near_vort = sums[0:3]
    near_curl = sums[3:6]
    grad_vort = sums[6:9]
    grad_curl = sums[9:12]
    grad_outer_vort = sums[12:21].reshape(3, 3, count)
    grad_outer_curl = sums[21:30].reshape(3, 3, count)
    velocity = -strength * (jnp.cross(where_pos, near_vort, axis=0) - near_curl)
    along = jnp.sum(where_vort * where_pos, axis=0)
    first_term = along[None, :] * (jnp.cross(where_pos, grad_vort, axis=0) - grad_curl)
    inside = jnp.cross(where_pos[None, :, :], grad_outer_vort, axis=1) - grad_outer_curl
    second_term = jnp.sum(where_vort[:, None, :] * inside, axis=0)
    stretch = -strength * (jnp.cross(where_vort, near_vort, axis=0) + first_term - second_term)
    return (velocity, stretch)


def buckets(mig_pos, mig_vort, mig_valid, routing, groups, capacity):
    destinations = 2 * groups
    matches = (routing[:, 0][:, None] == jnp.arange(destinations, dtype=jnp.int32)[None, :]).astype(
        jnp.int32
    )
    before = jnp.cumsum(matches, axis=0) - matches
    order_in = jnp.sum(before * matches, axis=1)
    slot_index = routing[:, 0] * capacity + order_in
    placing = (
        slot_index[:, None] == jnp.arange(destinations * capacity, dtype=jnp.int32)[None, :]
    ).astype(jnp.float32)
    record = jnp.concatenate([mig_pos, mig_vort, mig_valid.astype(jnp.float32)[None, :]], axis=0)
    placed = jnp.dot(record, placing, precision=highest, preferred_element_type=jnp.float32)
    return placed.reshape(7, 2, groups, capacity)


def frame_table():
    first = (jnp.arange(7, dtype=jnp.int32) == 0).astype(jnp.float32)[:, None]
    sides = jnp.array([-1.0, 1.0], dtype=jnp.float32)[None, :]
    return first * sides


def per_device(
    src_pos, src_vort, face_valid, tgt_pos, tgt_vort, mig_pos, mig_vort, mig_valid, mig_route
):
    groups = lax.axis_size("grp")
    places = src_pos[0, 0]
    vortex = src_vort[0, 0]
    sources = places.shape[1]
    face_count = face_valid.shape[3]
    face_masks = face_valid[0, 0].astype(jnp.float32)
    along_jet = (jnp.arange(3, dtype=jnp.int32) == 0).astype(jnp.float32)[:, None]
    filled = buckets(mig_pos[0, 0], mig_vort[0, 0], mig_valid[0, 0], mig_route[0, 0], groups, CAP)
    members = lax.all_to_all(filled, "grp", split_axis=2, concat_axis=2, tiled=True)
    padded = padded_2(members, (("slab", 1),), 1)
    arrived = jnp.stack([padded[:, 0], padded[:, 3]], axis=1)
    arrived = arrived + frame_table()[:, :, None, None]
    where_pos = jnp.concatenate([tgt_pos[0, 0], arrived[0:3].reshape(3, -1)], axis=1)
    where_vort = jnp.concatenate([tgt_vort[0, 0], arrived[3:6].reshape(3, -1)], axis=1)
    living = jnp.concatenate(
        [jnp.ones((tgt_pos.shape[3],), jnp.float32), arrived[6].reshape(-1)], axis=0
    )
    own_rows = expand(places, vortex)
    slab_all, slab_masks = (
        lax.all_gather(own_rows, "grp", axis=1, tiled=True),
        lax.all_gather(face_masks, "grp", axis=1, tiled=True),
    )
    vort_start = 4
    spread = slab_all.reshape(slab_all.shape[0], groups, sources)
    low_pos = spread[0:3, :, :face_count].reshape(3, -1) + along_jet
    low_vort = (
        spread[vort_start : vort_start + 3, :, :face_count].reshape(3, -1) * slab_masks[0][None, :]
    )
    high_pos = spread[0:3, :, sources - face_count :].reshape(3, -1) - along_jet
    high_vort = (
        spread[vort_start : vort_start + 3, :, sources - face_count :].reshape(3, -1)
        * slab_masks[1][None, :]
    )
    record = jnp.stack([expand(low_pos, low_vort), expand(high_pos, high_vort)], axis=1)
    padded_faces = padded_2(record, (("slab", 1),), 1)
    received = jnp.concatenate([padded_faces[:, 0], padded_faces[:, 3]], axis=1)
    blocks = (jnp.concatenate([slab_all, received], axis=1),)
    for substep in range(STEPS):
        velocity, stretch = rates_from(where_pos, where_vort, blocks)
        where_pos = where_pos + time_step * velocity
        where_vort = where_vort + time_step * stretch
    moved_pos = (where_pos * living[None, :])[None, None]
    moved_vort = (where_vort * living[None, :])[None, None]
    return (moved_pos, moved_vort)


def solution(mesh):
    return jax.shard_map(
        per_device,
        mesh=mesh,
        in_specs=(
            P("slab", "grp", None, None),
            P("slab", "grp", None, None),
            P("slab", "grp", None, None),
            P("slab", "grp", None, None),
            P("slab", "grp", None, None),
            P("slab", "grp", None, None),
            P("slab", "grp", None, None),
            P("slab", "grp", None),
            P("slab", "grp", None, None),
        ),
        out_specs=(P("slab", "grp", None, None), P("slab", "grp", None, None)),
        check_vma=False,
    )
```

profile of v0, /device:TPU:9, one launch (start us, length us, event | category | flops | bytes accessed | tf_op | source)
XLA Modules:
  0.0 671.2 jit_solution(18435817935249034052)
XLA Ops:
  9.4 6.1 concatenate.55
  17.1 27.5 %all-gather = f32[1,1,2,16384]{3,2,1,0:T(2,128)S(1)} all-gather(f32[1,1,2,2048]{3,2,1,0:T(2,128)S(1)} %convert_element_type.48), channel_id=2, replica_groups=mesh['slab'=16,'grp'=8] {'grp'}, dimensions={3}, use_global_device_ids=true | all-gather | bytes 147456 | tf_op jit(solution)/shard_map/all_gather | solution.py:140
  47.4 61.9 %all-gather.3.cloned.1.call-done = f32[28,32768]{1,0:T(8,128)} async-done(((f32[28,4096]{1,0:T(8,128)}), f32[28,32768]{1,0:T(8,128)}) %all-gather.3.cloned.1.call-update) | async-done | bytes 3670032 | tf_op jit(solution)/shard_map/all_gather | solution.py:139
  119.5 12.3 %concatenate.56 = f32[28,16384]{1,0:T(8,128)S(1)} concatenate(f32[3,16384]{1,0:T(4,128)} %copy-done, f32[1,16384]{1,0:T(1,128)S(1)} %bitcast.243, f32[3,16384]{1,0:T(4,128)} %copy-done.3, f32[3,16384]{1,0:T(4,128)} %copy-done.1, f32[9,16384]{1,0:T(8,128)} %mul.702, f32[9,16384]{1,0:T(8,128)S(1)} %mul.705), dimensions={0} | concatenate | bytes 3670016 | tf_op jit(solution)/shard_map/concatenate | solution.py:40
  139.5 12.2 %concatenate.57 = f32[28,16384]{1,0:T(8,128)S(1)} concatenate(f32[3,16384]{1,0:T(4,128)S(1)} %get-tuple-element.336, f32[1,16384]{1,0:T(1,128)S(1)} %bitcast.242, f32[3,16384]{1,0:T(4,128)} %broadcast_multiply_fusion.4, f32[3,16384]{1,0:T(4,128)} %copy-done.2, f32[9,16384]{1,0:T(8,128)} %mul.713, f32[9,16384]{1,0:T(8,128)S(1)} %mul.716), dimensions={0} | concatenate | bytes 3670016 | tf_op jit(solution)/shard_map/concatenate | solution.py:40
  165.8 34.9 %all-to-all-done = f32[7,2,8,8]{3,1,0,2:T(2,128)S(1)} async-done(((f32[7,2,8,8]{3,1,0,2:T(2,128)}), f32[7,2,8,8]{3,1,0,2:T(2,128)S(1)}, u32[]{:S(2)}, u32[]{:S(2)}) %all-to-all-start) | async-done | bytes 3616 | tf_op jit(solution)/shard_map/all_to_all | solution.py:128
  219.4 217.6 %while.28 = (s32[]{:T(128)}, f32[30,256]{1,0:T(8,128)S(1)}, f32[28,65536]{1,0:T(8,128)}, f32[256]{0:T(256)S(1)}, f32[3,256]{1,0:T(4,128)S(1)}, /*index=5*/s32[]{...) while((s32[]{:T(128)}, f32[30,256]{1,0:T(8,128)S(1)}, f32[28,65536]{1,0:T(8,128)}, ...), condition=%wide.region_7.9_spmd.clone, body=%wide.region_6.8_spmd.clone.sunk | while | flops 1736464896 | bytes 53014744 | solution.py:72
  221.2 20.3 %fusion.133 = f32[16384,256]{1,0:T(8,128)S(1)} fusion(f32[3,256]{1,0:T(4,128)S(1)} %get-tuple-element.431, f32[256]{0:T(256)S(1)} %get-tuple-element.430, f32[16384]{0:T(1024)S(1)} %bitcast.223, f32[28,65536]{1,0:T(8,128)} %get-tuple-element.429, s32[]{:T(128)S(6)} %select_n.18), kind=kOutput, calls=%fused_computation.3.clone.1 | convolution fusion | flops 163577856 | bytes 17108996 | tf_op jit(solution)/shard_map/while/body/eval_jaxpr/dot_general | solution.py:51
  241.5 15.1 %fusion.135 = f32[6,256]{1,0:T(8,128)S(1)} fusion(f32[16384,256]{1,0:T(8,128)S(1)} %fusion.133, f32[28,65536]{1,0:T(8,128)} %get-tuple-element.429, s32[]{:T(128)S(6)} %add.372, s32[]{:T(128)S(6)} %select_n.18), kind=kOutput, calls=%fused_computation.5.clone.1 | convolution fusion | flops 327155712 | bytes 17307656 | tf_op jit(solution)/shard_map/while/body/eval_jaxpr/dot_general | solution.py:63
  256.6 16.9 %fusion.134 = f32[24,256]{1,0:T(8,128)S(1)} fusion(f32[16384,256]{1,0:T(8,128)S(1)} %fusion.133, f32[28,65536]{1,0:T(8,128)} %get-tuple-element.429, s32[]{:T(128)S(6)} %add.372, s32[]{:T(128)S(6)} %select_n.18), kind=kOutput, calls=%fused_computation.7.clone.1 | convolution fusion | flops 1245708288 | bytes 18374664 | tf_op jit(solution)/shard_map/while/body/eval_jaxpr/dot_general | solution.py:66
  275.3 20.3 %fusion.133 = f32[16384,256]{1,0:T(8,128)S(1)} fusion(f32[3,256]{1,0:T(4,128)S(1)} %get-tuple-element.431, f32[256]{0:T(256)S(1)} %get-tuple-element.430, f32[16384]{0:T(1024)S(1)} %bitcast.223, f32[28,65536]{1,0:T(8,128)} %get-tuple-element.429, s32[]{:T(128)S(6)} %select_n.18), kind=kOutput, calls=%fused_computation.3.clone.1 | convolution fusion | flops 163577856 | bytes 17108996 | tf_op jit(solution)/shard_map/while/body/eval_jaxpr/dot_general | solution.py:51
  295.5 15.1 %fusion.135 = f32[6,256]{1,0:T(8,128)S(1)} fusion(f32[16384,256]{1,0:T(8,128)S(1)} %fusion.133, f32[28,65536]{1,0:T(8,128)} %get-tuple-element.429, s32[]{:T(128)S(6)} %add.372, s32[]{:T(128)S(6)} %select_n.18), kind=kOutput, calls=%fused_computation.5.clone.1 | convolution fusion | flops 327155712 | bytes 17307656 | tf_op jit(solution)/shard_map/while/body/eval_jaxpr/dot_general | solution.py:63
  310.7 16.9 %fusion.134 = f32[24,256]{1,0:T(8,128)S(1)} fusion(f32[16384,256]{1,0:T(8,128)S(1)} %fusion.133, f32[28,65536]{1,0:T(8,128)} %get-tuple-element.429, s32[]{:T(128)S(6)} %add.372, s32[]{:T(128)S(6)} %select_n.18), kind=kOutput, calls=%fused_computation.7.clone.1 | convolution fusion | flops 1245708288 | bytes 18374664 | tf_op jit(solution)/shard_map/while/body/eval_jaxpr/dot_general | solution.py:66
  329.3 20.3 %fusion.133 = f32[16384,256]{1,0:T(8,128)S(1)} fusion(f32[3,256]{1,0:T(4,128)S(1)} %get-tuple-element.431, f32[256]{0:T(256)S(1)} %get-tuple-element.430, f32[16384]{0:T(1024)S(1)} %bitcast.223, f32[28,65536]{1,0:T(8,128)} %get-tuple-element.429, s32[]{:T(128)S(6)} %select_n.18), kind=kOutput, calls=%fused_computation.3.clone.1 | convolution fusion | flops 163577856 | bytes 17108996 | tf_op jit(solution)/shard_map/while/body/eval_jaxpr/dot_general | solution.py:51
  349.6 15.1 %fusion.135 = f32[6,256]{1,0:T(8,128)S(1)} fusion(f32[16384,256]{1,0:T(8,128)S(1)} %fusion.133, f32[28,65536]{1,0:T(8,128)} %get-tuple-element.429, s32[]{:T(128)S(6)} %add.372, s32[]{:T(128)S(6)} %select_n.18), kind=kOutput, calls=%fused_computation.5.clone.1 | convolution fusion | flops 327155712 | bytes 17307656 | tf_op jit(solution)/shard_map/while/body/eval_jaxpr/dot_general | solution.py:63
  364.7 16.9 %fusion.134 = f32[24,256]{1,0:T(8,128)S(1)} fusion(f32[16384,256]{1,0:T(8,128)S(1)} %fusion.133, f32[28,65536]{1,0:T(8,128)} %get-tuple-element.429, s32[]{:T(128)S(6)} %add.372, s32[]{:T(128)S(6)} %select_n.18), kind=kOutput, calls=%fused_computation.7.clone.1 | convolution fusion | flops 1245708288 | bytes 18374664 | tf_op jit(solution)/shard_map/while/body/eval_jaxpr/dot_general | solution.py:66
  383.3 20.3 %fusion.133 = f32[16384,256]{1,0:T(8,128)S(1)} fusion(f32[3,256]{1,0:T(4,128)S(1)} %get-tuple-element.431, f32[256]{0:T(256)S(1)} %get-tuple-element.430, f32[16384]{0:T(1024)S(1)} %bitcast.223, f32[28,65536]{1,0:T(8,128)} %get-tuple-element.429, s32[]{:T(128)S(6)} %select_n.18), kind=kOutput, calls=%fused_computation.3.clone.1 | convolution fusion | flops 163577856 | bytes 17108996 | tf_op jit(solution)/shard_map/while/body/eval_jaxpr/dot_general | solution.py:51
  403.6 15.1 %fusion.135 = f32[6,256]{1,0:T(8,128)S(1)} fusion(f32[16384,256]{1,0:T(8,128)S(1)} %fusion.133, f32[28,65536]{1,0:T(8,128)} %get-tuple-element.429, s32[]{:T(128)S(6)} %add.372, s32[]{:T(128)S(6)} %select_n.18), kind=kOutput, calls=%fused_computation.5.clone.1 | convolution fusion | flops 327155712 | bytes 17307656 | tf_op jit(solution)/shard_map/while/body/eval_jaxpr/dot_general | solution.py:63
  418.7 16.9 %fusion.134 = f32[24,256]{1,0:T(8,128)S(1)} fusion(f32[16384,256]{1,0:T(8,128)S(1)} %fusion.133, f32[28,65536]{1,0:T(8,128)} %get-tuple-element.429, s32[]{:T(128)S(6)} %add.372, s32[]{:T(128)S(6)} %select_n.18), kind=kOutput, calls=%fused_computation.7.clone.1 | convolution fusion | flops 1245708288 | bytes 18374664 | tf_op jit(solution)/shard_map/while/body/eval_jaxpr/dot_general | solution.py:66
  439.2 223.6 %while.29 = (s32[]{:T(128)}, f32[30,256]{1,0:T(8,128)S(1)}, f32[28,65536]{1,0:T(8,128)}, f32[256]{0:T(256)S(1)}, f32[3,256]{1,0:T(4,128)S(1)}, /*index=5*/s32[]{...) while((s32[]{:T(128)}, f32[30,256]{1,0:T(8,128)S(1)}, f32[28,65536]{1,0:T(8,128)}, ...), condition=%wide.region_10.13_spmd.clone, body=%wide.region_9.12_spmd.clone.sunk | while | flops 1736464896 | bytes 53014744 | solution.py:72
  446.9 20.5 %fusion.142 = f32[16384,256]{1,0:T(8,128)S(1)} fusion(f32[3,256]{1,0:T(4,128)S(1)} %get-tuple-element.464, f32[256]{0:T(256)S(1)} %get-tuple-element.463, f32[16384]{0:T(1024)S(1)} %bitcast.224, f32[28,65536]{1,0:T(8,128)} %get-tuple-element.462, s32[]{:T(128)S(6)} %select_n.19), kind=kOutput, calls=%fused_computation.37.clone.1 | convolution fusion | flops 163577856 | bytes 17108996 | tf_op jit(solution)/shard_map/while/body/eval_jaxpr/dot_general | solution.py:51
  467.4 14.9 %fusion.144 = f32[6,256]{1,0:T(8,128)S(1)} fusion(f32[16384,256]{1,0:T(8,128)S(1)} %fusion.142, f32[28,65536]{1,0:T(8,128)} %get-tuple-element.462, s32[]{:T(128)S(6)} %add.384, s32[]{:T(128)S(6)} %select_n.19), kind=kOutput, calls=%fused_computation.39.clone.1 | convolution fusion | flops 327155712 | bytes 17307656 | tf_op jit(solution)/shard_map/while/body/eval_jaxpr/dot_general | solution.py:63
  482.3 17.2 %fusion.143 = f32[24,256]{1,0:T(8,128)S(1)} fusion(f32[16384,256]{1,0:T(8,128)S(1)} %fusion.142, f32[28,65536]{1,0:T(8,128)} %get-tuple-element.462, s32[]{:T(128)S(6)} %add.384, s32[]{:T(128)S(6)} %select_n.19), kind=kOutput, calls=%fused_computation.41.clone.1 | convolution fusion | flops 1245708288 | bytes 18374664 | tf_op jit(solution)/shard_map/while/body/eval_jaxpr/dot_general | solution.py:66
  500.9 20.3 %fusion.142 = f32[16384,256]{1,0:T(8,128)S(1)} fusion(f32[3,256]{1,0:T(4,128)S(1)} %get-tuple-element.464, f32[256]{0:T(256)S(1)} %get-tuple-element.463, f32[16384]{0:T(1024)S(1)} %bitcast.224, f32[28,65536]{1,0:T(8,128)} %get-tuple-element.462, s32[]{:T(128)S(6)} %select_n.19), kind=kOutput, calls=%fused_computation.37.clone.1 | convolution fusion | flops 163577856 | bytes 17108996 | tf_op jit(solution)/shard_map/while/body/eval_jaxpr/dot_general | solution.py:51
  521.2 15.2 %fusion.144 = f32[6,256]{1,0:T(8,128)S(1)} fusion(f32[16384,256]{1,0:T(8,128)S(1)} %fusion.142, f32[28,65536]{1,0:T(8,128)} %get-tuple-element.462, s32[]{:T(128)S(6)} %add.384, s32[]{:T(128)S(6)} %select_n.19), kind=kOutput, calls=%fused_computation.39.clone.1 | convolution fusion | flops 327155712 | bytes 17307656 | tf_op jit(solution)/shard_map/while/body/eval_jaxpr/dot_general | solution.py:63
  536.4 16.9 %fusion.143 = f32[24,256]{1,0:T(8,128)S(1)} fusion(f32[16384,256]{1,0:T(8,128)S(1)} %fusion.142, f32[28,65536]{1,0:T(8,128)} %get-tuple-element.462, s32[]{:T(128)S(6)} %add.384, s32[]{:T(128)S(6)} %select_n.19), kind=kOutput, calls=%fused_computation.41.clone.1 | convolution fusion | flops 1245708288 | bytes 18374664 | tf_op jit(solution)/shard_map/while/body/eval_jaxpr/dot_general | solution.py:66
  555.0 20.3 %fusion.142 = f32[16384,256]{1,0:T(8,128)S(1)} fusion(f32[3,256]{1,0:T(4,128)S(1)} %get-tuple-element.464, f32[256]{0:T(256)S(1)} %get-tuple-element.463, f32[16384]{0:T(1024)S(1)} %bitcast.224, f32[28,65536]{1,0:T(8,128)} %get-tuple-element.462, s32[]{:T(128)S(6)} %select_n.19), kind=kOutput, calls=%fused_computation.37.clone.1 | convolution fusion | flops 163577856 | bytes 17108996 | tf_op jit(solution)/shard_map/while/body/eval_jaxpr/dot_general | solution.py:51
  575.3 15.1 %fusion.144 = f32[6,256]{1,0:T(8,128)S(1)} fusion(f32[16384,256]{1,0:T(8,128)S(1)} %fusion.142, f32[28,65536]{1,0:T(8,128)} %get-tuple-element.462, s32[]{:T(128)S(6)} %add.384, s32[]{:T(128)S(6)} %select_n.19), kind=kOutput, calls=%fused_computation.39.clone.1 | convolution fusion | flops 327155712 | bytes 17307656 | tf_op jit(solution)/shard_map/while/body/eval_jaxpr/dot_general | solution.py:63
  590.4 16.9 %fusion.143 = f32[24,256]{1,0:T(8,128)S(1)} fusion(f32[16384,256]{1,0:T(8,128)S(1)} %fusion.142, f32[28,65536]{1,0:T(8,128)} %get-tuple-element.462, s32[]{:T(128)S(6)} %add.384, s32[]{:T(128)S(6)} %select_n.19), kind=kOutput, calls=%fused_computation.41.clone.1 | convolution fusion | flops 1245708288 | bytes 18374664 | tf_op jit(solution)/shard_map/while/body/eval_jaxpr/dot_general | solution.py:66
  609.1 20.3 %fusion.142 = f32[16384,256]{1,0:T(8,128)S(1)} fusion(f32[3,256]{1,0:T(4,128)S(1)} %get-tuple-element.464, f32[256]{0:T(256)S(1)} %get-tuple-element.463, f32[16384]{0:T(1024)S(1)} %bitcast.224, f32[28,65536]{1,0:T(8,128)} %get-tuple-element.462, s32[]{:T(128)S(6)} %select_n.19), kind=kOutput, calls=%fused_computation.37.clone.1 | convolution fusion | flops 163577856 | bytes 17108996 | tf_op jit(solution)/shard_map/while/body/eval_jaxpr/dot_general | solution.py:51
  629.4 15.1 %fusion.144 = f32[6,256]{1,0:T(8,128)S(1)} fusion(f32[16384,256]{1,0:T(8,128)S(1)} %fusion.142, f32[28,65536]{1,0:T(8,128)} %get-tuple-element.462, s32[]{:T(128)S(6)} %add.384, s32[]{:T(128)S(6)} %select_n.19), kind=kOutput, calls=%fused_computation.39.clone.1 | convolution fusion | flops 327155712 | bytes 17307656 | tf_op jit(solution)/shard_map/while/body/eval_jaxpr/dot_general | solution.py:63
  644.5 16.9 %fusion.143 = f32[24,256]{1,0:T(8,128)S(1)} fusion(f32[16384,256]{1,0:T(8,128)S(1)} %fusion.142, f32[28,65536]{1,0:T(8,128)} %get-tuple-element.462, s32[]{:T(128)S(6)} %add.384, s32[]{:T(128)S(6)} %select_n.19), kind=kOutput, calls=%fused_computation.41.clone.1 | convolution fusion | flops 1245708288 | bytes 18374664 | tf_op jit(solution)/shard_map/while/body/eval_jaxpr/dot_general | solution.py:66
  (158 shorter events, 70.4 us)
Async XLA Ops:
  7.2 102.2 %all-gather.3.cloned.1.call-start = ((), (), s32[]{:S(2)}) async-start(), calls=%async_computation.1 | async-start | bytes 4718592 | tf_op jit(solution)/shard_map/all_gather | solution.py:139
  114.7 4.8 copy-start.3
  116.9 48.8 %copy-start.19 = (f32[1,1,3,128]{3,1,2,0:T(1,128)S(1)}, f32[1,1,3,128]{3,1,2,0:T(1,128)}, u32[]{:S(2)}) copy-start(f32[1,1,3,128]{3,1,2,0:T(1,128)} %param.24) | copy-start | bytes 4612
  117.0 48.8 %copy-start.20 = (f32[1,1,3,128]{3,1,2,0:T(1,128)S(1)}, f32[1,1,3,128]{3,1,2,0:T(1,128)}, u32[]{:S(2)}) copy-start(f32[1,1,3,128]{3,1,2,0:T(1,128)} %param.23) | copy-start | bytes 4612
  117.1 0.8 copy-start
  117.6 1.9 copy-start.1
  136.6 2.9 copy-start.2
  154.9 55.6 %collective-permute-start.3 = (f32[28,1,16384]{2,1,0:T(1,128)}, f32[28,1,16384]{2,1,0:T(1,128)}, u32[]{:S(2)}, u32[]{:S(2)}) collective-permute-start(f32[28,1,16384]{2,1,0:T(1,128)} %stack.11), channel_id=1, source_target_pairs={{8,0},{16,8},{24,16},{32,24},{40,32},{48,40},{56,48},{64,56},{72,6... | collective-permute-start | bytes 5505032 | tf_op jit(solution)/shard_map/ppermute | solution.py:27
  155.4 57.7 %collective-permute-start.2 = (f32[28,1,16384]{2,1,0:T(1,128)}, f32[28,1,16384]{2,1,0:T(1,128)S(1)}, u32[]{:S(2)}, u32[]{:S(2)}) collective-permute-start(f32[28,1,16384]{2,1,0:T(1,128)} %stack.10), channel_id=1, source_target_pairs={{0,8},{8,16},{16,24},{24,32},{32,40},{40,48},{48,56},{56,64},{64,7... | collective-permute-start | bytes 5505032 | tf_op jit(solution)/shard_map/ppermute | solution.py:25
  160.4 40.3 %all-to-all-start = ((f32[7,2,8,8]{3,1,0,2:T(2,128)}), f32[7,2,8,8]{3,1,0,2:T(2,128)S(1)}, u32[]{:S(2)}, u32[]{:S(2)}) async-start(f32[7,2,8,8]{3,1,0,2:T(2,128)} %copy.14), calls=%async_computation | async-start | bytes 114688 | tf_op jit(solution)/shard_map/all_to_all | solution.py:128
  165.8 53.6 %copy-start.7 = (f32[3,128]{1,0:T(4,128)}, f32[3,128]{1,0:T(4,128)S(1)}, u32[]{:S(2)}) copy-start(f32[3,128]{1,0:T(4,128)S(1)} %get-tuple-element.341) | copy-start | bytes 4612
  165.8 53.6 %copy-start.8 = (f32[3,128]{1,0:T(4,128)}, f32[3,128]{1,0:T(4,128)S(1)}, u32[]{:S(2)}) copy-start(f32[3,128]{1,0:T(4,128)S(1)} %get-tuple-element.342) | copy-start | bytes 4612
  200.7 3.1 collective-permute-start
  202.9 4.8 collective-permute-start.1
  207.9 11.5 %copy-start.9 = (f32[3,128]{1,0:T(4,128)}, f32[3,128]{1,0:T(4,128)S(1)}, u32[]{:S(2)}) copy-start(f32[3,128]{1,0:T(4,128)S(1)} %reshape.800) | copy-start | bytes 4612
  208.1 11.3 %copy-start.10 = (f32[3,128]{1,0:T(4,128)}, f32[3,128]{1,0:T(4,128)S(1)}, u32[]{:S(2)}) copy-start(f32[3,128]{1,0:T(4,128)S(1)} %reshape.806) | copy-start | bytes 4612
  219.3 217.8 %copy-start.12 = (f32[256,3]{0,1:T(4,128)S(1)}, f32[256,3]{0,1:T(4,128)}, u32[]{:S(2)}) copy-start(f32[256,3]{0,1:T(4,128)} %get-tuple-element.327) | copy-start | bytes 9220
  219.3 217.8 %copy-start.6 = (f32[256,3]{0,1:T(4,128)S(1)}, f32[256,3]{0,1:T(4,128)}, u32[]{:S(2)}) copy-start(f32[256,3]{0,1:T(4,128)} %get-tuple-element.328) | copy-start | bytes 9220
  219.3 217.9 %copy-start.16 = (f32[1,256,1]{1,2,0:T(1,128)S(1)}, f32[1,256,1]{1,2,0:T(1,128)}, u32[]{:S(2)}) copy-start(f32[1,256,1]{1,2,0:T(1,128)} %get-tuple-element.332) | copy-start | bytes 3076
  219.3 217.9 %copy-start.17 = (f32[1,256,1]{1,2,0:T(1,128)S(1)}, f32[1,256,1]{1,2,0:T(1,128)}, u32[]{:S(2)}) copy-start(f32[1,256,1]{1,2,0:T(1,128)} %get-tuple-element.333) | copy-start | bytes 3076
  219.3 217.9 %copy-start.18 = (f32[1,256,1]{1,2,0:T(1,128)S(1)}, f32[1,256,1]{1,2,0:T(1,128)}, u32[]{:S(2)}) copy-start(f32[1,256,1]{1,2,0:T(1,128)} %get-tuple-element.334) | copy-start | bytes 3076
  219.4 217.9 %copy-start.11 = (f32[3,256]{1,0:T(4,128)S(1)}, f32[3,256]{1,0:T(4,128)}, u32[]{:S(2)}) copy-start(f32[3,256]{1,0:T(4,128)} %get-tuple-element.331) | copy-start | bytes 9220
  219.4 217.9 %copy-start.13 = (f32[256]{0:T(256)S(1)}, f32[256]{0:T(256)}, u32[]{:S(2)}) copy-start(f32[256]{0:T(256)} %get-tuple-element.237) | copy-start | bytes 3076
  219.4 219.8 %copy-start.4 = (f32[30,256]{1,0:T(8,128)S(1)}, f32[30,256]{1,0:T(8,128)}, u32[]{:S(2)}) copy-start(f32[30,256]{1,0:T(8,128)} %custom-call.1) | copy-start | bytes 92164
  439.2 223.7 %copy-start.5 = (f32[3,256]{1,0:T(4,128)S(1)}, f32[3,256]{1,0:T(4,128)}, u32[]{:S(2)}) copy-start(f32[3,256]{1,0:T(4,128)} %get-tuple-element.259) | copy-start | bytes 9220
  439.2 223.8 %copy-start.14 = (f32[256]{0:T(256)S(1)}, f32[256]{0:T(256)}, u32[]{:S(2)}) copy-start(f32[256]{0:T(256)} %get-tuple-element.235) | copy-start | bytes 3076
  439.2 223.8 %copy-start.15 = (f32[256]{0:T(256)S(1)}, f32[256]{0:T(256)}, u32[]{:S(2)}) copy-start(f32[256]{0:T(256)} %concatenate.59) | copy-start | bytes 3076
Sparse Core Ops, SparseCore 0:
  15.6 93.6 all-gather.2
where the time goes:
time: 683 us; the launch traced here: 671 us
  matrix products  420 us (61%)
  waiting for transfers between devices  101 us (15%)
  local copies, waits for them, and re-layouts  64.9 us (10%)
  blocking collectives  27.5 us (4%)
  other arithmetic  20.3 us (3%)
  between operations  14.9 us (2%)
  loops' own time  12.2 us (2%)
  starting transfers between devices  10.8 us (2%)
    dot_general x8, matrix products, one_block(): lax.dot_general(block[0:3], where_pos, (((0,), (0,)), ((), ())), precisio...  162 us
    dot_general x8, matrix products, one_block(): jnp.dot(block[4:28], fweight, precision=highest, preferred_element_type=j...  136 us
    dot_general x8, matrix products, one_block(): jnp.dot(block[4:10], qweight, precision=highest, preferred_element_type=j...  121 us
    all_gather x1, waiting for transfers between devices, per_device(): lax.all_gather(own_rows, 'grp', axis=1, tiled=True)  61.9 us
    all_to_all x1, waiting for transfers between devices, per_device(): lax.all_to_all(filled, 'grp', split_axis=2, concat_axis=2, tiled=True)  34.9 us
    concatenate x3, local copies, waits for them, and re-layouts, expand(): jnp.concatenate([places, squares, vortex, curled, outer_vort, outer_curl]...  30.5 us
    all_gather x1, blocking collectives, per_device(): lax.all_gather(face_masks, 'grp', axis=1, tiled=True)  27.5 us
  transfers between devices with their start and end apart: 6, of which 4 were waited for; matrix products, arithmetic and copies ran while one was open for 2% of the time, Pallas kernels for 0%

commit v1 on v0

v1 whole, which is shorter than its diff:
```python
import functools
import math

import jax
import jax.numpy as jnp
from jax import lax
from jax.experimental import pallas as pl
from jax.experimental.pallas import tpu as pltpu
from jax.sharding import PartitionSpec as P

CAP = 8
STEPS = 2
core_square = 0.0225
time_step = 0.1
strength = 0.03 / (4.0 * math.pi)
highest = lax.Precision.HIGHEST

centre = 0.5
unit_square = 1.5 * core_square
unit = math.sqrt(unit_square)
velocity_factor = -strength / unit_square
stretch_factor = -strength / (unit_square * unit)
f32 = jnp.float32
bf16 = jnp.bfloat16
BLOCK = 4096


def three_pieces(values):
    high = values.astype(bf16).astype(f32)
    rest = values - high
    middle = rest.astype(bf16).astype(f32)
    low = rest - middle
    return high, middle, low


def prepare_kernel(pos_ref, vort_ref, near_ref, grad_ref, dist_ref, rows, dist):
    places = [(pos_ref[k : k + 1, :] - centre) * (1.0 / unit) for k in range(3)]
    vortex = [vort_ref[k : k + 1, :] for k in range(3)]
    curled = [
        places[(k + 1) % 3] * vortex[(k + 2) % 3] - places[(k + 2) % 3] * vortex[(k + 1) % 3]
        for k in range(3)
    ]
    for k in range(3):
        rows[k : k + 1, :] = vortex[k]
        rows[3 + k : 4 + k, :] = curled[k]
        for l in range(3):
            at = 6 + 3 * k + l
            rows[at : at + 1, :] = places[k] * vortex[l]
            rows[at + 9 : at + 10, :] = places[k] * curled[l]
    high, middle, low = three_pieces(rows[...])
    blank = jnp.zeros((8, high.shape[1]), f32)
    grad_ref[...] = jnp.concatenate([high, middle, low, blank], axis=0).astype(bf16)
    near_ref[...] = jnp.concatenate([high[0:8], middle[0:8], low[0:8], blank], axis=0).astype(bf16)
    square = places[0] * places[0] + places[1] * places[1] + places[2] * places[2]
    square_parts = three_pieces(square + core_square / unit_square)
    dist[...] = jnp.zeros_like(dist)
    for k in range(3):
        parts = three_pieces(places[k])
        for place, part in enumerate((0, 0, 1, 0, 2, 1)):
            dist[3 * place + k : 3 * place + k + 1, :] = parts[part]
        dist[18 + k : 19 + k, :] = square_parts[k]
        dist[21 + k : 22 + k, :] = jnp.ones_like(square)
    dist_ref[...] = dist[...].astype(bf16)


def prepare(places, vortex):
    length = places.shape[1]
    whole = pl.BlockSpec(memory_space=pltpu.VMEM)
    return pl.pallas_call(
        prepare_kernel,
        in_specs=[whole, whole],
        out_specs=[whole, whole, whole],
        out_shape=[
            jax.ShapeDtypeStruct((32, length), bf16),
            jax.ShapeDtypeStruct((80, length), bf16),
            jax.ShapeDtypeStruct((32, length), bf16),
        ],
        scratch_shapes=[pltpu.VMEM((24, length), f32), pltpu.VMEM((32, length), f32)],
        compiler_params=pltpu.CompilerParams(vmem_limit_bytes=48 << 20),
    )(places, vortex)


def two_pieces(values):
    high = values.astype(bf16)
    low = (values - high.astype(f32)).astype(bf16)
    return jnp.concatenate([high, low], axis=0)


def dot(left, right):
    return lax.dot_general(left, right, (((1,), (0,)), ((), ())), preferred_element_type=f32)


def cross(left, right):
    return [
        left[(k + 1) % 3] * right[(k + 2) % 3] - left[(k + 2) % 3] * right[(k + 1) % 3]
        for k in range(3)
    ]


def pairs_kernel(tgt_ref, near_ref, grad_ref, dist_ref, out_ref, tgt, near_sums, grad_sums):
    where = [(tgt_ref[0, k : k + 1, :] - centre) * (1.0 / unit) for k in range(3)]
    vortex = [tgt_ref[0, 3 + k : 4 + k, :] for k in range(3)]
    square = where[0] * where[0] + where[1] * where[1] + where[2] * where[2]
    square_parts = three_pieces(square)
    tgt[...] = jnp.zeros_like(tgt)
    for k in range(3):
        parts = three_pieces(-2.0 * where[k])
        for place, part in enumerate((0, 1, 0, 2, 0, 1)):
            tgt[3 * place + k : 3 * place + k + 1, :] = parts[part]
        tgt[18 + k : 19 + k, :] = jnp.ones_like(square)
        tgt[21 + k : 22 + k, :] = square_parts[k]
    targets = tgt[...].astype(bf16)
    near_sums[...] = jnp.zeros_like(near_sums)
    grad_sums[...] = jnp.zeros_like(grad_sums)
    length = near_ref.shape[1]
    width = min(BLOCK, length)

    def one_block(index, carry):
        piece = pl.ds(pl.multiple_of(index * width, width), width)
        distance = lax.dot_general(
            dist_ref[:, piece], targets, (((0,), (0,)), ((), ())), preferred_element_type=f32
        )
        root = lax.rsqrt(distance)
        square_inv = root * root
        third = square_inv * root
        fifth = third * square_inv
        qweight = two_pieces(third + fifth)
        fweight = two_pieces(fifth * (square_inv + 0.6))
        near = near_ref[:, piece]
        grad = grad_ref[:, piece]
        near_sums[...] += dot(jnp.concatenate([near, near], axis=1), qweight)
        grad_sums[...] += dot(jnp.concatenate([grad, grad], axis=1), fweight)
        return carry

    lax.fori_loop(0, length // width, one_block, 0)
    near = near_sums[0:8, :] + near_sums[8:16, :] + near_sums[16:24, :]
    grad = grad_sums[0:24, :] + grad_sums[24:48, :] + grad_sums[48:72, :]

    def three(values, first):
        return [values[first + k : first + k + 1, :] for k in range(3)]

    near_vort, near_curl = three(near, 0), three(near, 3)
    grad_vort, grad_curl = three(grad, 0), three(grad, 3)
    turned = cross(where, near_vort)
    velocity = [velocity_factor * (turned[k] - near_curl[k]) for k in range(3)]
    along = vortex[0] * where[0] + vortex[1] * where[1] + vortex[2] * where[2]
    turned = cross(where, grad_vort)
    inner = [along * (turned[k] - grad_curl[k]) for k in range(3)]
    for axis in range(3):
        turned = cross(where, three(grad, 6 + 3 * axis))
        outer = three(grad, 15 + 3 * axis)
        inner = [inner[k] - vortex[axis] * (turned[k] - outer[k]) for k in range(3)]
    turned = cross(vortex, near_vort)
    out_ref[...] = jnp.zeros_like(out_ref)
    for k in range(3):
        out_ref[0, k : k + 1, :] = velocity[k]
        out_ref[0, 3 + k : 4 + k, :] = stretch_factor * (turned[k] - 5.0 * inner[k])


def pair_sums(table, near, grad, dist):
    tiles, rows, width = table.shape
    whole = pl.BlockSpec(memory_space=pltpu.VMEM)
    return pl.pallas_call(
        pairs_kernel,
        grid=(tiles,),
        in_specs=[pl.BlockSpec((1, rows, width), lambda i: (i, 0, 0)), whole, whole, whole],
        out_specs=pl.BlockSpec((1, rows, width), lambda i: (i, 0, 0)),
        out_shape=jax.ShapeDtypeStruct(table.shape, f32),
        scratch_shapes=[
            pltpu.VMEM((32, width), f32),
            pltpu.VMEM((32, width), f32),
            pltpu.VMEM((80, width), f32),
        ],
        compiler_params=pltpu.CompilerParams(vmem_limit_bytes=56 << 20),
    )(table, near, grad, dist)


def buckets(mig_pos, mig_vort, mig_valid, routing, groups, capacity):
    destinations = 2 * groups
    matches = (routing[:, 0][:, None] == jnp.arange(destinations, dtype=jnp.int32)[None, :]).astype(
        jnp.int32
    )
    before = jnp.cumsum(matches, axis=0) - matches
    order_in = jnp.sum(before * matches, axis=1)
    slot_index = routing[:, 0] * capacity + order_in
    placing = (
        slot_index[:, None] == jnp.arange(destinations * capacity, dtype=jnp.int32)[None, :]
    ).astype(f32)
    record = jnp.concatenate([mig_pos, mig_vort, mig_valid.astype(f32)[None, :]], axis=0)
    placed = jnp.dot(record, placing, precision=highest, preferred_element_type=f32)
    return placed.reshape(7, 2, groups * capacity)


def swap(values):
    return lax.all_to_all(values, "grp", split_axis=0, concat_axis=0, tiled=True)


def spread(values, groups):
    return swap(jnp.broadcast_to(values[None], (groups,) + values.shape))


def per_device(
    src_pos, src_vort, face_valid, tgt_pos, tgt_vort, mig_pos, mig_vort, mig_valid, mig_route
):
    groups = lax.axis_size("grp")
    slabs = lax.axis_size("slab")
    member = lax.axis_index("grp")
    places = src_pos[0, 0]
    vortex = src_vort[0, 0]
    sources = places.shape[1]
    faces = face_valid.shape[3]
    own = tgt_pos.shape[3]
    masks = face_valid[0, 0].astype(f32)
    along_jet = (jnp.arange(3, dtype=jnp.int32) == 0).astype(f32)[:, None]
    filled = buckets(mig_pos[0, 0], mig_vort[0, 0], mig_valid[0, 0], mig_route[0, 0], groups, CAP)
    slots = filled.shape[2]
    shift = (jnp.arange(7, dtype=jnp.int32) == 0).astype(f32)[:, None]
    going_up = jnp.concatenate(
        [
            jnp.concatenate([places[:, sources - faces :] - along_jet], axis=0).reshape(-1),
            (vortex[:, sources - faces :] * masks[1][None]).reshape(-1),
            (filled[:, 1] - shift).reshape(-1),
        ]
    )
    going_down = jnp.concatenate(
        [
            (places[:, :faces] + along_jet).reshape(-1),
            (vortex[:, :faces] * masks[0][None]).reshape(-1),
            (filled[:, 0] + shift).reshape(-1),
        ]
    )
    from_lower = lax.ppermute(going_up, "slab", [(i, (i + 1) % slabs) for i in range(slabs)])
    from_upper = lax.ppermute(going_down, "slab", [((i + 1) % slabs, i) for i in range(slabs)])
    arrived = jnp.stack([from_lower[6 * faces :], from_upper[6 * faces :]])
    arrived = arrived.reshape(2, 7, groups, CAP).transpose(1, 2, 0, 3).reshape(-1)
    sent = jnp.concatenate([tgt_pos[0, 0].reshape(-1), tgt_vort[0, 0].reshape(-1), arrived])
    table = spread(sent.reshape(-1, 128), groups).reshape(groups, -1)
    own_part = table[:, : 6 * own].reshape(groups, 6, own)
    own_part = jnp.concatenate(
        [own_part, jnp.ones((groups, 1, own), f32), jnp.zeros((groups, 1, own), f32)], axis=1
    )
    slot_part = table[:, 6 * own :].reshape(groups, 7, groups, 2, CAP).transpose(2, 1, 3, 0, 4)
    slot_part = slot_part.reshape(groups, 7, 2 * groups * CAP)
    slot_part = jnp.pad(slot_part, ((0, 0), (0, 1), (0, 0)))
    table = jnp.concatenate([own_part, slot_part], axis=2)

    all_places = jnp.concatenate(
        [places, from_lower[: 3 * faces].reshape(3, faces), from_upper[: 3 * faces].reshape(3, faces)],
        axis=1,
    )
    all_vortex = jnp.concatenate(
        [
            vortex,
            from_lower[3 * faces : 6 * faces].reshape(3, faces),
            from_upper[3 * faces : 6 * faces].reshape(3, faces),
        ],
        axis=1,
    )
    near, grad, dist = prepare(all_places, all_vortex)
    mine = lax.dynamic_index_in_dim(table, member, 0, keepdims=False)
    living = mine[6:7]
    for substep in range(STEPS):
        if substep > 0:
            table = spread(mine, groups)
        partial = swap(pair_sums(table, near, grad, dist))
        mine = mine + time_step * jnp.sum(partial, axis=0)
    moved_pos = (mine[0:3] * living)[None, None]
    moved_vort = (mine[3:6] * living)[None, None]
    return (moved_pos, moved_vort)


def solution(mesh):
    return jax.shard_map(
        per_device,
        mesh=mesh,
        in_specs=(
            P("slab", "grp", None, None),
            P("slab", "grp", None, None),
            P("slab", "grp", None, None),
            P("slab", "grp", None, None),
            P("slab", "grp", None, None),
            P("slab", "grp", None, None),
            P("slab", "grp", None, None),
            P("slab", "grp", None),
            P("slab", "grp", None, None),
        ),
        out_specs=(P("slab", "grp", None, None), P("slab", "grp", None, None)),
        check_vma=False,
    )
```

time: 683 us -> 157 us (0.23)
  the two profiles are of different devices: /device:TPU:9 before, /device:TPU:0 now
where the time goes in v1:
time: 157 us; the launch traced here: 156 us
  Pallas kernels  89.6 us (57%)
  waiting for transfers between devices  27.2 us (17%)
  starting transfers between devices  20.7 us (13%)
  local copies, waits for them, and re-layouts  10.9 us (7%)
  other arithmetic  6.15 us (4%)
    pallas_call x2, Pallas kernels, pair_sums(): pl.pallas_call(pairs_kernel, grid=(tiles,), in_specs=[pl.BlockSpec((1, ro...  88.6 us
    all_to_all x4, waiting for transfers between devices, swap(): lax.all_to_all(values, 'grp', split_axis=0, concat_axis=0, tiled=True)  20.2 us
    all_to_all x4, starting transfers between devices, swap(): lax.all_to_all(values, 'grp', split_axis=0, concat_axis=0, tiled=True)  15 us
    unnamed x18, local copies, waits for them, and re-layouts  6.87 us
    ppermute x1, starting transfers between devices, per_device(): lax.ppermute(going_down, 'slab', [((i + 1) % slabs, i) for i in range(sla...  5.66 us
    ppermute x1, waiting for transfers between devices, per_device(): lax.ppermute(going_up, 'slab', [(i, (i + 1) % slabs) for i in range(slabs)])  5.4 us
  transfers between devices with their start and end apart: 6, of which 6 were waited for; matrix products, arithmetic and copies ran while one was open for 1% of the time, Pallas kernels for 1%

profile of v1, /device:TPU:0, one launch (start us, length us, event | category | flops | bytes accessed | tf_op | source)
XLA Modules:
  0.0 155.7 jit_solution(10144552411043732766)
XLA Ops:
  0.7 0.7 fusion
  1.5 0.8 select_reduce_fusion
  2.4 0.7 multiply_add_fusion
  3.1 0.7 convert_bitcast_fusion
  3.7 0.7 copy_bitcast_fusion.3
  5.0 0.8 copy.40
  5.9 0.7 convert_element_type.42
  6.7 0.8 copy.41
  7.7 5.7 %collective-permute-start.1 = (f32[12736]{0:T(1024)S(1)}, f32[12736]{0:T(1024)S(1)}, u32[]{:S(2)}, u32[]{:S(2)}) collective-permute-start(f32[12736]{0:T(1024)S(1)} %pad_maximum_fusion.3), channel_id=1, source_target_pairs={{8,0},{16,8},{24,16},{32,24},{40,32},{48,40},{56,48},{64,56},{72,6... | collective-permute-start | bytes 152840 | tf_op jit(solution)/shard_map/ppermute | solution.py:233
  13.6 1.5 collective-permute-done.1
  15.2 5.4 %collective-permute-done = f32[12736]{0:T(1024)S(1)} collective-permute-done((f32[12736]{0:T(1024)S(1)}, f32[12736]{0:T(1024)S(1)}, u32[]{:S(2)}, u32[]{:S(2)}) %collective-permute-start) | collective-permute-done | bytes 50976 | tf_op jit(solution)/shard_map/ppermute | solution.py:232
  21.0 0.6 broadcast_in_dim.34
  21.6 4.9 %all-to-all-start = ((f32[8,13,128]{2,1,0:T(8,128)}), f32[8,13,128]{2,1,0:T(8,128)S(1)}, u32[]{:S(2)}, u32[]{:S(2)}) async-start(f32[8,13,128]{2,1,0:T(8,128)} %broadcast_in_dim.34), calls=%async_computation | async-start | bytes 131072 | tf_op jit(solution)/shard_map/all_to_all | solution.py:195
  26.7 1.1 shard_map.104
  27.8 1.1 copy-done
  28.8 0.8 copy-done.1
  29.6 0.8 copy-done.2
  30.5 2.3 %all-to-all-done = f32[8,13,128]{2,1,0:T(8,128)S(1)} async-done(((f32[8,13,128]{2,1,0:T(8,128)}), f32[8,13,128]{2,1,0:T(8,128)S(1)}, u32[]{:S(2)}, u32[]{:S(2)}) %all-to-all-start) | async-done | bytes 53280 | tf_op jit(solution)/shard_map/all_to_all | solution.py:195
  32.8 0.7 reshape.112
  33.9 0.6 select_maximum_fusion.tgt_ref
  34.6 44.3 %shard_map.105 = f32[8,8,256]{2,1,0:T(8,128)} custom-call(f32[8,8,256]{2,1,0:T(8,128)} %select_maximum_fusion.tgt_ref, bf16[32,8192]{1,0:T(8,128)(2,1)} %copy-done.1, bf16[80,8192]{1,0:T(8,128)(2,1)} %copy-done, bf16[32,8192]{1,0:T(8,128)(2,1)} %copy-done.2), custom_call_target="tpu_custom_call" | custom-call | tf_op jit(solution)/shard_map/pallas_call | solution.py:163
  78.9 3.4 %all-to-all-start.1 = ((f32[8,8,256]{2,1,0:T(8,128)}), f32[8,8,256]{2,1,0:T(8,128)S(1)}, u32[]{:S(2)}, u32[]{:S(2)}) async-start(f32[8,8,256]{2,1,0:T(8,128)} %shard_map.105), calls=%async_computation.1 | async-start | bytes 131072 | tf_op jit(solution)/shard_map/all_to_all | solution.py:195
  82.2 6.3 %all-to-all-done.1 = f32[8,8,256]{2,1,0:T(8,128)S(1)} async-done(((f32[8,8,256]{2,1,0:T(8,128)}), f32[8,8,256]{2,1,0:T(8,128)S(1)}, u32[]{:S(2)}, u32[]{:S(2)}) %all-to-all-start.1) | async-done | bytes 65568 | tf_op jit(solution)/shard_map/all_to_all | solution.py:195
  88.5 0.7 fusion.3
  89.2 0.6 broadcast_in_dim.38
  89.8 3.3 %all-to-all-start.2 = ((f32[8,8,256]{2,1,0:T(8,128)}), f32[8,8,256]{2,1,0:T(8,128)S(1)}, u32[]{:S(2)}, u32[]{:S(2)}) async-start(f32[8,8,256]{2,1,0:T(8,128)} %broadcast_in_dim.38), calls=%async_computation.2 | async-start | bytes 131072 | tf_op jit(solution)/shard_map/all_to_all | solution.py:195
  93.2 6.2 %all-to-all-done.2.tgt_ref = f32[8,8,256]{2,1,0:T(8,128)S(1)} async-done(((f32[8,8,256]{2,1,0:T(8,128)}), f32[8,8,256]{2,1,0:T(8,128)S(1)}, u32[]{:S(2)}, u32[]{:S(2)}) %all-to-all-start.2) | async-done | bytes 65568 | tf_op jit(solution)/shard_map/all_to_all | solution.py:195
  100.0 44.3 %shard_map.106 = f32[8,8,256]{2,1,0:T(8,128)} custom-call(f32[8,8,256]{2,1,0:T(8,128)} %copy-done.3, bf16[32,8192]{1,0:T(8,128)(2,1)} %copy-done.1, bf16[80,8192]{1,0:T(8,128)(2,1)} %copy-done, bf16[32,8192]{1,0:T(8,128)(2,1)} %copy-done.2), custom_call_target="tpu_custom_call" | custom-call | tf_op jit(solution)/shard_map/pallas_call | solution.py:163
  144.3 3.3 %all-to-all-start.3 = ((f32[8,8,256]{2,1,0:T(8,128)}), f32[8,8,256]{2,1,0:T(8,128)S(1)}, u32[]{:S(2)}, u32[]{:S(2)}) async-start(f32[8,8,256]{2,1,0:T(8,128)} %shard_map.106), calls=%async_computation.3 | async-start | bytes 131072 | tf_op jit(solution)/shard_map/all_to_all | solution.py:195
  147.7 0.7 constant_dynamic-slice_fusion
  148.4 5.5 %all-to-all-done.3 = f32[8,8,256]{2,1,0:T(8,128)S(1)} async-done(((f32[8,8,256]{2,1,0:T(8,128)}), f32[8,8,256]{2,1,0:T(8,128)S(1)}, u32[]{:S(2)}, u32[]{:S(2)}) %all-to-all-start.3) | async-done | bytes 65568 | tf_op jit(solution)/shard_map/all_to_all | solution.py:195
  153.9 0.7 fusion.4
  (62 shorter events, 3.9 us)
Async XLA Ops:
  0.6 12.8 %copy-start.4 = (f32[1,1,3,128]{3,1,2,0:T(1,128)S(1)}, f32[1,1,3,128]{3,1,2,0:T(1,128)}, u32[]{:S(2)}) copy-start(f32[1,1,3,128]{3,1,2,0:T(1,128)} %param.13) | copy-start | bytes 4612
  0.6 12.9 %copy-start.5 = (f32[1,1,3,128]{3,1,2,0:T(1,128)S(1)}, f32[1,1,3,128]{3,1,2,0:T(1,128)}, u32[]{:S(2)}) copy-start(f32[1,1,3,128]{3,1,2,0:T(1,128)} %param.12) | copy-start | bytes 4612
  7.7 7.5 %collective-permute-start.1 = (f32[12736]{0:T(1024)S(1)}, f32[12736]{0:T(1024)S(1)}, u32[]{:S(2)}, u32[]{:S(2)}) collective-permute-start(f32[12736]{0:T(1024)S(1)} %pad_maximum_fusion.3), channel_id=1, source_target_pairs={{8,0},{16,8},{24,16},{32,24},{40,32},{48,40},{56,48},{64,56},{72,6... | collective-permute-start | bytes 152840 | tf_op jit(solution)/shard_map/ppermute | solution.py:233
  13.4 7.2 %collective-permute-start = (f32[12736]{0:T(1024)S(1)}, f32[12736]{0:T(1024)S(1)}, u32[]{:S(2)}, u32[]{:S(2)}) collective-permute-start(f32[12736]{0:T(1024)S(1)} %pad_maximum_fusion.2), channel_id=1, source_target_pairs={{0,8},{8,16},{16,24},{24,32},{32,40},{40,48},{48,56},{56,64},{64,7... | collective-permute-start | bytes 152840 | tf_op jit(solution)/shard_map/ppermute | solution.py:232
  21.6 11.2 %all-to-all-start = ((f32[8,13,128]{2,1,0:T(8,128)}), f32[8,13,128]{2,1,0:T(8,128)S(1)}, u32[]{:S(2)}, u32[]{:S(2)}) async-start(f32[8,13,128]{2,1,0:T(8,128)} %broadcast_in_dim.34), calls=%async_computation | async-start | bytes 131072 | tf_op jit(solution)/shard_map/all_to_all | solution.py:195
  27.8 1.1 copy-start
  28.8 0.8 copy-start.1
  29.6 0.8 copy-start.2
  78.9 9.6 %all-to-all-start.1 = ((f32[8,8,256]{2,1,0:T(8,128)}), f32[8,8,256]{2,1,0:T(8,128)S(1)}, u32[]{:S(2)}, u32[]{:S(2)}) async-start(f32[8,8,256]{2,1,0:T(8,128)} %shard_map.105), calls=%async_computation.1 | async-start | bytes 131072 | tf_op jit(solution)/shard_map/all_to_all | solution.py:195
  89.8 9.5 %all-to-all-start.2 = ((f32[8,8,256]{2,1,0:T(8,128)}), f32[8,8,256]{2,1,0:T(8,128)S(1)}, u32[]{:S(2)}, u32[]{:S(2)}) async-start(f32[8,8,256]{2,1,0:T(8,128)} %broadcast_in_dim.38), calls=%async_computation.2 | async-start | bytes 131072 | tf_op jit(solution)/shard_map/all_to_all | solution.py:195
  99.4 0.6 copy-start.3
  144.3 9.5 %all-to-all-start.3 = ((f32[8,8,256]{2,1,0:T(8,128)}), f32[8,8,256]{2,1,0:T(8,128)S(1)}, u32[]{:S(2)}, u32[]{:S(2)}) async-start(f32[8,8,256]{2,1,0:T(8,128)} %shard_map.106), calls=%async_computation.3 | async-start | bytes 131072 | tf_op jit(solution)/shard_map/all_to_all | solution.py:195

commit v2 on v1

v2 whole, which is shorter than its diff:
```python
import functools
import math

import jax
import jax.numpy as jnp
from jax import lax
from jax.experimental import pallas as pl
from jax.experimental.pallas import tpu as pltpu
from jax.sharding import PartitionSpec as P

CAP = 8
STEPS = 2
core_square = 0.0225
time_step = 0.1
strength = 0.03 / (4.0 * math.pi)

centre = 0.5
unit_square = 1.5 * core_square
unit = math.sqrt(unit_square)
velocity_factor = -strength / unit_square
stretch_factor = -strength / (unit_square * unit)
f32 = jnp.float32
bf16 = jnp.bfloat16
whole = pl.BlockSpec(memory_space=pltpu.VMEM)


def three_pieces(values):
    high = values.astype(bf16).astype(f32)
    rest = values - high
    middle = rest.astype(bf16).astype(f32)
    low = rest - middle
    return high, middle, low


def two_pieces(values):
    high = values.astype(bf16)
    low = (values - high.astype(f32)).astype(bf16)
    return jnp.concatenate([high, low], axis=0)


def dot(left, right):
    return lax.dot_general(left, right, (((1,), (0,)), ((), ())), preferred_element_type=f32)


def cross(left, right):
    return [
        left[(k + 1) % 3] * right[(k + 2) % 3] - left[(k + 2) % 3] * right[(k + 1) % 3]
        for k in range(3)
    ]


def send_kernel(
    faces, pos_ref, vort_ref, valid_ref, mig_pos_ref, mig_vort_ref, mig_valid_ref, route_ref,
    up_ref, down_ref, record,
):
    sources = pos_ref.shape[1]
    migrants = route_ref.shape[0]
    slots = (up_ref.shape[1] - faces) // 2
    destinations = 2 * slots // CAP
    route = route_ref[...]
    matches = route == lax.broadcasted_iota(jnp.int32, (migrants, destinations), 1)
    matches = jnp.where(matches, 1.0, 0.0)
    earlier = lax.broadcasted_iota(jnp.int32, (migrants, migrants), 0) > lax.broadcasted_iota(
        jnp.int32, (migrants, migrants), 1
    )
    before = dot(jnp.where(earlier, 1.0, 0.0).astype(bf16), matches.astype(bf16))
    order = jnp.sum(before * matches, axis=1, keepdims=True).astype(jnp.int32)
    placing = (route * CAP + order) == lax.broadcasted_iota(jnp.int32, (migrants, 2 * slots), 1)
    placing = jnp.where(placing, 1.0, 0.0).astype(bf16)
    record[...] = jnp.zeros_like(record)
    record[0:3, :] = mig_pos_ref[...]
    record[3:6, :] = mig_vort_ref[...]
    record[6:7, :] = mig_valid_ref[...].astype(f32)
    pieces = jnp.concatenate(three_pieces(record[...]), axis=0)
    placed = dot(jnp.concatenate([pieces, jnp.zeros((8, migrants), f32)], axis=0).astype(bf16), placing)
    placed = placed[0:8] + placed[8:16] + placed[16:24]
    first = lax.broadcasted_iota(jnp.int32, placed.shape, 0) == 0
    for ref, begin, shift, which in ((down_ref, 0, 1.0, 0), (up_ref, sources - faces, -1.0, 1)):
        piece = slice(begin, begin + faces)
        mask = valid_ref[which : which + 1, :].astype(f32)
        ref[0:1, :faces] = pos_ref[0:1, piece] + shift
        ref[1:3, :faces] = pos_ref[1:3, piece]
        ref[3:6, :faces] = vort_ref[:, piece] * mask
        ref[6:8, :faces] = jnp.zeros((2, faces), f32)
        ref[:, faces:] = jnp.where(first, placed + shift, placed)


def make_sends(places, vortex, valid, mig_pos, mig_vort, mig_valid, route, destinations):
    faces = valid.shape[1]
    shape = jax.ShapeDtypeStruct((8, faces + destinations * CAP), f32)
    return pl.pallas_call(
        functools.partial(send_kernel, faces),
        in_specs=[whole] * 7,
        out_specs=[whole] * 2,
        out_shape=[shape, shape],
        scratch_shapes=[pltpu.VMEM((8, route.shape[0]), f32)],
        compiler_params=pltpu.CompilerParams(vmem_limit_bytes=48 << 20),
    )(places, vortex, valid, mig_pos, mig_vort, mig_valid, route)


def prepare_kernel(length, *refs):
    source_refs = refs[:-5]
    near_ref, grad_ref, dist_ref, rows, dist = refs[-5:]

    def columns(row):
        if source_refs[0].shape[0] == 3:
            return source_refs[row // 3][row % 3 : row % 3 + 1, :]
        return jnp.concatenate([ref[row : row + 1, : length // 2] for ref in source_refs], axis=1)

    places = [(columns(k) - centre) * (1.0 / unit) for k in range(3)]
    vortex = [columns(3 + k) for k in range(3)]
    curled = cross(places, vortex)
    for k in range(3):
        rows[k : k + 1, :] = vortex[k]
        rows[3 + k : 4 + k, :] = curled[k]
        for l in range(3):
            at = 6 + 3 * k + l
            rows[at : at + 1, :] = places[k] * vortex[l]
            rows[at + 9 : at + 10, :] = places[k] * curled[l]
    high, middle, low = three_pieces(rows[...])
    blank = jnp.zeros((8, high.shape[1]), f32)
    grad_ref[...] = jnp.concatenate([high, middle, low, blank], axis=0).astype(bf16)
    near_ref[...] = jnp.concatenate([high[0:8], middle[0:8], low[0:8], blank], axis=0).astype(bf16)
    square = places[0] * places[0] + places[1] * places[1] + places[2] * places[2]
    square_parts = three_pieces(square + core_square / unit_square)
    dist[...] = jnp.zeros_like(dist)
    for k in range(3):
        parts = three_pieces(places[k])
        for place, part in enumerate((0, 0, 1, 0, 2, 1)):
            dist[3 * place + k : 3 * place + k + 1, :] = parts[part]
        dist[18 + k : 19 + k, :] = square_parts[k]
        dist[21 + k : 22 + k, :] = jnp.ones_like(square)
    dist_ref[...] = dist[...].astype(bf16)


def prepare(length, *sources):
    return pl.pallas_call(
        functools.partial(prepare_kernel, length),
        in_specs=[whole] * len(sources),
        out_specs=[whole] * 3,
        out_shape=[
            jax.ShapeDtypeStruct((32, length), bf16),
            jax.ShapeDtypeStruct((80, length), bf16),
            jax.ShapeDtypeStruct((32, length), bf16),
        ],
        scratch_shapes=[pltpu.VMEM((24, length), f32), pltpu.VMEM((32, length), f32)],
        compiler_params=pltpu.CompilerParams(vmem_limit_bytes=48 << 20),
    )(*sources)


def compact_kernel(arrived_ref, table_ref, rank_ref, count_ref):
    groups, _, slots = arrived_ref.shape
    valid = jnp.concatenate([arrived_ref[m, 14:15, :] for m in range(groups)], axis=0)
    row = lax.broadcasted_iota(jnp.int32, (slots, slots), 0)
    column = lax.broadcasted_iota(jnp.int32, (slots, slots), 1)
    earlier = jnp.where(row < column, 1.0, 0.0).astype(bf16)
    same = jnp.where(row == column, 1.0, 0.0).astype(bf16)

    def turned(matrix, which):
        return lax.dot_general(
            matrix, which, (((0,), (1,)), ((), ())), preferred_element_type=f32
        )

    flags = valid.astype(bf16)
    within = turned(earlier, flags)
    living = turned(same, flags)
    totals = jnp.sum(living, axis=0, keepdims=True)
    ahead = [jnp.zeros((1, 1), f32)]
    for m in range(1, groups):
        ahead.append(ahead[-1] + totals[:, m - 1 : m])
    rank = jnp.where(living > 0.5, within + jnp.concatenate(ahead, axis=1), -1.0)
    rank_ref[...] = rank
    count_ref[0, 0] = jnp.sum(valid).astype(jnp.int32)
    wanted = lax.broadcasted_iota(jnp.int32, (slots, groups * slots), 1).astype(f32)
    placed = jnp.zeros((32, groups * slots), f32)
    for m in range(groups):
        pieces = three_pieces(arrived_ref[m, 8:16, :])
        pieces = jnp.concatenate(pieces + (jnp.zeros((8, slots), f32),), axis=0).astype(bf16)
        chosen = jnp.where(rank[:, m : m + 1] == wanted, 1.0, 0.0).astype(bf16)
        placed = placed + dot(pieces, chosen)
    placed = placed[0:8] + placed[8:16] + placed[16:24]
    for m in range(groups):
        table_ref[m] = placed[:, m * slots : (m + 1) * slots]


def compact(received):
    groups, _, slots = received.shape
    return pl.pallas_call(
        compact_kernel,
        in_specs=[whole],
        out_specs=[whole, whole, pl.BlockSpec(memory_space=pltpu.SMEM)],
        out_shape=[
            jax.ShapeDtypeStruct((groups, 8, slots), f32),
            jax.ShapeDtypeStruct((slots, groups), f32),
            jax.ShapeDtypeStruct((1, 1), jnp.int32),
        ],
        compiler_params=pltpu.CompilerParams(vmem_limit_bytes=48 << 20),
    )(received)


def expand_kernel(rank_ref, own_ref, moved_ref, table_ref, sums_ref, places_ref):
    groups, _, slots = moved_ref.shape
    rows = [
        jnp.concatenate([ref[m] for m in range(groups)], axis=1) for ref in (moved_ref, table_ref)
    ]
    pieces = jnp.concatenate(three_pieces(jnp.concatenate(rows, axis=0)), axis=0).astype(bf16)
    wanted = lax.broadcasted_iota(jnp.int32, (slots, groups * slots), 1).astype(f32)
    for member in range(groups):
        chosen = jnp.where(rank_ref[:, member : member + 1] == wanted, 1.0, 0.0).astype(bf16)
        found = lax.dot_general(
            pieces, chosen, (((1,), (1,)), ((), ())), preferred_element_type=f32
        )
        found = found[0:16] + found[16:32] + found[32:48]
        sums_ref[member, 0:8, :] = own_ref[member]
        sums_ref[member, 8:16, :] = found[0:8]
        places_ref[member] = found[8:16]


def expand_slots(rank, own, moved, table):
    groups, _, slots = moved.shape
    return pl.pallas_call(
        expand_kernel,
        in_specs=[whole] * 4,
        out_specs=[whole] * 2,
        out_shape=[
            jax.ShapeDtypeStruct((groups, 16, slots), f32),
            jax.ShapeDtypeStruct((groups, 8, slots), f32),
        ],
        compiler_params=pltpu.CompilerParams(vmem_limit_bytes=48 << 20),
    )(rank, own, moved, table)


def finish_kernel(member_ref, sums_ref, own_ref, slot_ref, pos_ref, vort_ref):
    member = member_ref[0]
    total = sums_ref[0]
    for sender in range(1, sums_ref.shape[0]):
        total = total + sums_ref[sender]
    width = own_ref.shape[2]
    for at, ref in ((0, own_ref), (1, slot_ref)):
        table = ref[member]
        result = (table + time_step * total[8 * at : 8 * at + 8]) * table[6:7]
        lanes = slice(at * width, at * width + width)
        pos_ref[0, 0, :, lanes] = result[0:3]
        vort_ref[0, 0, :, lanes] = result[3:6]


def finish(member, sums, own, slots):
    shape = jax.ShapeDtypeStruct((1, 1, 3, 2 * own.shape[2]), f32)
    return pl.pallas_call(
        finish_kernel,
        in_specs=[pl.BlockSpec(memory_space=pltpu.SMEM), whole, whole, whole],
        out_specs=[whole] * 2,
        out_shape=[shape, shape],
    )(member.reshape(1), sums, own, slots)


CHUNK = 128
FINE = 32
SLOTS = 6
AHEAD = 3


def pairs_kernel(sets, moved, copies, counted, *refs):
    refs = list(refs)
    count_ref = refs.pop(0) if counted else None
    tgt_ref = refs.pop(0)
    moved_ref = refs.pop(0) if moved else None
    source_refs = [refs.pop(0) for _ in range(3 * sets)]
    out_ref = refs.pop(0)
    table_ref = refs.pop(0) if moved else None
    tgt, near_sums, grad_sums = refs[:3]
    held = refs[3:]
    halves, rows, half = tgt_ref.shape

    def run():
        def joined(ref):
            return jnp.concatenate([ref[0], ref[1]], axis=1)

        table = joined(tgt_ref)
        if moved:
            step = joined(moved_ref.at[0])
            for sender in range(1, moved_ref.shape[0]):
                step = step + joined(moved_ref.at[sender])
            table = table + time_step * step
            table_ref[0] = table[:, :half]
            table_ref[1] = table[:, half:]
        where = [(table[k : k + 1, :] - centre) * (1.0 / unit) for k in range(3)]
        vortex = [table[3 + k : 4 + k, :] for k in range(3)]
        square = where[0] * where[0] + where[1] * where[1] + where[2] * where[2]
        square_parts = three_pieces(square)
        tgt[...] = jnp.zeros_like(tgt)
        for k in range(3):
            parts = three_pieces(-2.0 * where[k])
            for place, part in enumerate((0, 1, 0, 2, 0, 1)):
                tgt[3 * place + k : 3 * place + k + 1, :] = parts[part]
            tgt[18 + k : 19 + k, :] = jnp.ones_like(square)
            tgt[21 + k : 22 + k, :] = square_parts[k]
        targets = tgt[...].astype(bf16)
        near_sums[...] = jnp.zeros_like(near_sums)
        grad_sums[...] = jnp.zeros_like(grad_sums)
        start = jnp.minimum(pl.program_id(0), 0)
        per_set = source_refs[0].shape[1] // CHUNK
        chunks = sets * per_set

        def source(which, chunk):
            number, place = divmod(chunk, per_set)
            return source_refs[3 * number + which][:, place * CHUNK : (place + 1) * CHUNK]

        def read(ref, at, count):
            return ref[pl.ds(pl.multiple_of(start * CHUNK + at, count), count), :]

        def distances(chunk):
            held[chunk % SLOTS][...] = lax.dot_general(
                source(2, chunk), targets, (((0,), (0,)), ((), ())), preferred_element_type=f32
            )

        def weights(chunk):
            distance_ref = held[chunk % SLOTS]
            near_ref = held[SLOTS + chunk % SLOTS]
            grad_ref = held[2 * SLOTS + chunk % SLOTS]
            for at in range(0, CHUNK, FINE):
                root = lax.rsqrt(read(distance_ref, at, FINE))
                square_inv = root * root
                third = square_inv * root
                fifth = third * square_inv
                for ref, weight in (
                    (near_ref, third + fifth),
                    (grad_ref, fifth * (square_inv + 0.6)),
                ):
                    high = weight.astype(bf16)
                    ref[at : at + FINE, :] = high
                    ref[CHUNK + at : CHUNK + at + FINE, :] = (weight - high.astype(f32)).astype(bf16)

        def sums(chunk):
            for which, ref, total in ((0, held[SLOTS + chunk % SLOTS], near_sums), (1, held[2 * SLOTS + chunk % SLOTS], grad_sums)):
                terms = source(which, chunk)
                total[...] += dot(
                    jnp.concatenate([terms, terms], axis=1), read(ref, 0, 2 * CHUNK)
                )

        for chunk in range(AHEAD):
            distances(chunk)
        for chunk in range(chunks):
            if chunk + AHEAD < chunks:
                distances(chunk + AHEAD)
            if chunk >= AHEAD:
                sums(chunk - AHEAD)
            weights(chunk)
        for chunk in range(chunks - AHEAD, chunks):
            sums(chunk)
        near = near_sums[0:8, :] + near_sums[8:16, :] + near_sums[16:24, :]
        grad = grad_sums[0:24, :] + grad_sums[24:48, :] + grad_sums[48:72, :]

        def three(values, first):
            return [values[first + k : first + k + 1, :] for k in range(3)]

        near_vort, near_curl = three(near, 0), three(near, 3)
        grad_vort, grad_curl = three(grad, 0), three(grad, 3)
        turned = cross(where, near_vort)
        velocity = [velocity_factor * (turned[k] - near_curl[k]) for k in range(3)]
        along = vortex[0] * where[0] + vortex[1] * where[1] + vortex[2] * where[2]
        turned = cross(where, grad_vort)
        inner = [along * (turned[k] - grad_curl[k]) for k in range(3)]
        for axis in range(3):
            turned = cross(where, three(grad, 6 + 3 * axis))
            outer = three(grad, 15 + 3 * axis)
            inner = [inner[k] - vortex[axis] * (turned[k] - outer[k]) for k in range(3)]
        turned = cross(vortex, near_vort)
        stretch = [stretch_factor * (turned[k] - 5.0 * inner[k]) for k in range(3)]
        blank = jnp.zeros((2, 2 * half), f32)
        result = jnp.concatenate(velocity + stretch + [blank], axis=0)
        for copy in range(copies):
            out_ref[copy, 0] = result[:, :half]
            out_ref[copy, 1] = result[:, half:]

    if not counted:
        run()
        return
    used = pl.program_id(0) * 2 * half < count_ref[0, 0]
    pl.when(used)(run)

    @pl.when(jnp.logical_not(used))
    def _():
        out_ref[...] = jnp.zeros_like(out_ref)
        if moved:
            table_ref[...] = jnp.zeros_like(table_ref)


def pair_sums(table, source_sets, copies, moved=None, count=None):
    tiles, _, width = table.shape
    rows = 8
    pair = pl.BlockSpec((2, rows, width), lambda i: (i, 0, 0))
    operands, in_specs = [], []
    if count is not None:
        operands.append(count)
        in_specs.append(pl.BlockSpec(memory_space=pltpu.SMEM))
    operands.append(table)
    in_specs.append(pair)
    if moved is not None:
        operands.append(moved)
        in_specs.append(pl.BlockSpec((moved.shape[0], 2, rows, width), lambda i: (0, i, 0, 0)))
    sources = 0
    for source_set in source_sets:
        operands.extend(source_set)
        in_specs.extend([whole] * 3)
        sources += source_set[0].shape[1]
    out_shape = [jax.ShapeDtypeStruct((copies, tiles, rows, width), f32)]
    out_specs = [pl.BlockSpec((copies, 2, rows, width), lambda i: (0, i, 0, 0))]
    if moved is not None:
        out_shape.append(jax.ShapeDtypeStruct((tiles, rows, width), f32))
        out_specs.append(pair)
    pairs = sources * tiles * width
    return pl.pallas_call(
        functools.partial(pairs_kernel, len(source_sets), moved is not None, copies, count is not None),
        grid=(tiles // 2,),
        in_specs=in_specs,
        out_specs=out_specs,
        out_shape=out_shape,
        scratch_shapes=[
            pltpu.VMEM((32, 2 * width), f32),
            pltpu.VMEM((32, 2 * width), f32),
            pltpu.VMEM((80, 2 * width), f32),
        ]
        + [pltpu.VMEM((CHUNK, 2 * width), f32)] * SLOTS
        + [pltpu.VMEM((2 * CHUNK, 2 * width), bf16)] * (2 * SLOTS),
        compiler_params=pltpu.CompilerParams(vmem_limit_bytes=48 << 20),
        cost_estimate=pl.CostEstimate(
            flops=600 * pairs, bytes_accessed=300 * sources, transcendentals=pairs
        ),
    )(*operands)


def swap(values):
    return lax.all_to_all(values, "grp", split_axis=0, concat_axis=0, tiled=True)


def spread(values, groups):
    return swap(jnp.broadcast_to(values[None], (groups,) + values.shape))


def per_device(
    src_pos, src_vort, face_valid, tgt_pos, tgt_vort, mig_pos, mig_vort, mig_valid, mig_route
):
    groups = lax.axis_size("grp")
    slabs = lax.axis_size("slab")
    places = src_pos[0, 0]
    vortex = src_vort[0, 0]
    sources = places.shape[1]
    faces = face_valid.shape[3]
    own = tgt_pos.shape[3]
    slots = groups * CAP
    mine = jnp.concatenate(
        [tgt_pos[0, 0], tgt_vort[0, 0], jnp.ones((1, own), f32), jnp.zeros((1, own), f32)], axis=0
    )
    going_up, going_down = make_sends(
        places, vortex, face_valid[0, 0], mig_pos[0, 0], mig_vort[0, 0], mig_valid[0], mig_route[0, 0],
        2 * groups,
    )
    from_lower = lax.ppermute(going_up, "slab", [(i, (i + 1) % slabs) for i in range(slabs)])
    from_upper = lax.ppermute(going_down, "slab", [((i + 1) % slabs, i) for i in range(slabs)])
    own_set = prepare(sources, places, vortex)
    arrived = jnp.concatenate(
        [from_lower[:, faces + slots :], from_upper[:, faces : faces + slots]], axis=1
    )
    received = spread(jnp.concatenate([mine, arrived], axis=0), groups)
    face_set = prepare(2 * faces, from_lower, from_upper)
    sets = [own_set, face_set]
    (first_a,) = pair_sums(received, sets, groups)
    moved_a = swap(first_a.reshape(groups, -1, 128)).reshape(first_a.shape)
    table_b, rank, count = compact(received)
    (first_b,) = pair_sums(table_b, sets, groups, count=count)
    moved_b = swap(first_b.reshape(groups, -1, 128)).reshape(first_b.shape)
    second_a, table_a = pair_sums(received, sets, 1, moved=moved_a)
    second_b, table_b = pair_sums(table_b, sets, 1, moved=moved_b, count=count)
    rank = rank.reshape(2, groups, CAP, groups).transpose(0, 3, 2, 1).reshape(rank.shape)
    sums, table_b = expand_slots(rank, second_a[0], second_b[0], table_b)
    return finish(lax.axis_index("grp"), swap(sums), table_a, table_b)


def solution(mesh):
    return jax.shard_map(
        per_device,
        mesh=mesh,
        in_specs=(
            P("slab", "grp", None, None),
            P("slab", "grp", None, None),
            P("slab", "grp", None, None),
            P("slab", "grp", None, None),
            P("slab", "grp", None, None),
            P("slab", "grp", None, None),
            P("slab", "grp", None, None),
            P("slab", "grp", None),
            P("slab", "grp", None, None),
        ),
        out_specs=(P("slab", "grp", None, None), P("slab", "grp", None, None)),
        check_vma=False,
    )
```

time: 157 us -> 132 us (0.84)
  Pallas kernels: 89.6 us -> 80.4 us
  waiting for transfers between devices: 27.2 us -> 18.4 us
  other arithmetic: 6.15 us -> 0.08 us
  starting transfers between devices: 20.7 us -> 25.3 us
  local copies, waits for them, and re-layouts: 10.9 us -> 6.36 us
    pallas_call x3 -> x10, Pallas kernels: 89.6 us -> 80.4 us  [the longest x4 74.3 us: pair_sums(): pl.pallas_call(functools.partial(pairs_kernel, len(source_sets), moved is...]
    all_to_all x4, waiting for transfers between devices: 20.2 us -> 11.1 us  [swap(): lax.all_to_all(values, 'grp', split_axis=0, concat_axis=0, tiled=True)]
    all_to_all x4, starting transfers between devices: 15 us -> 19.6 us  [swap(): lax.all_to_all(values, 'grp', split_axis=0, concat_axis=0, tiled=True)]
    unnamed x18 -> x27, local copies, waits for them, and re-layouts: 6.87 us -> 3.56 us
    convert_element_type x5 -> x0, other arithmetic: 2.12 us -> none  [the longest x1 0.73 us: buckets(): (routing[:, 0][:, None] == jnp.arange(destinations, dtype=jnp.int32)[None...]
    pallas_call x0 -> x2, local copies, waits for them, and re-layouts: none -> 1.85 us  [finish(): pl.pallas_call(finish_kernel, in_specs=[pl.BlockSpec(memory_space=pltpu.S...]
  transfers between devices with their start and end apart: 6 -> 6, of which waited for: 6 -> 4; matrix products, arithmetic and copies ran while one was open for 1% -> 0% of each run, Pallas kernels for 1% -> 29%
where the time goes in v2:
time: 132 us; the launch traced here: 131 us
  Pallas kernels  80.4 us (61%)
  starting transfers between devices  25.3 us (19%)
  waiting for transfers between devices  18.4 us (14%)
  local copies, waits for them, and re-layouts  6.36 us (5%)
    pallas_call x4, Pallas kernels, pair_sums(): pl.pallas_call(functools.partial(pairs_kernel, len(source_sets), moved is...  74.3 us
    all_to_all x4, starting transfers between devices, swap(): lax.all_to_all(values, 'grp', split_axis=0, concat_axis=0, tiled=True)  19.6 us
    all_to_all x4, waiting for transfers between devices, swap(): lax.all_to_all(values, 'grp', split_axis=0, concat_axis=0, tiled=True)  11.1 us
    ppermute x1, starting transfers between devices, per_device(): lax.ppermute(going_down, 'slab', [((i + 1) % slabs, i) for i in range(sla...  5.64 us
    ppermute x1, waiting for transfers between devices, per_device(): lax.ppermute(going_up, 'slab', [(i, (i + 1) % slabs) for i in range(slabs)])  5.4 us
    unnamed x27, local copies, waits for them, and re-layouts  3.56 us
  transfers between devices with their start and end apart: 6, of which 4 were waited for; matrix products, arithmetic and copies ran while one was open for 0% of the time, Pallas kernels for 29%

profile of v2, /device:TPU:0, one launch (start us, length us, event | category | flops | bytes accessed | tf_op | source)
XLA Modules:
  0.0 131.3 jit_solution(6585829108697938687)
XLA Ops:
  0.6 0.6 copy-done.11
  1.3 0.1 copy.11.route_ref
  1.4 0.1 copy-done.5
  1.4 0.9 copy_bitcast_fusion
  2.4 0.7 copy-done.2
  3.1 0.5 shard_map.104
  3.6 5.6 %collective-permute-start.1 = (f32[8,2176]{1,0:T(8,128)S(1)}, f32[8,2176]{1,0:T(8,128)S(1)}, u32[]{:S(2)}, u32[]{:S(2)}) collective-permute-start(f32[8,2176]{1,0:T(8,128)S(1)} %get-tuple-element.20), channel_id=1, source_target_pairs={{8,0},{16,8},{24,16},{32,24},{40,32},{48,40},{56,48},{64,56},{72,6... | collective-permute-start | bytes 208904 | tf_op jit(solution)/shard_map/ppermute | solution.py:460
  9.2 1.9 %collective-permute-done.1.refs_1_ = f32[8,2176]{1,0:T(8,128)S(1)} collective-permute-done((f32[8,2176]{1,0:T(8,128)S(1)}, f32[8,2176]{1,0:T(8,128)S(1)}, u32[]{:S(2)}, u32[]{:S(2)}) %collective-permute-start.1) | collective-permute-done | bytes 69664 | tf_op jit(solution)/shard_map/ppermute | solution.py:460
  11.2 5.4 %collective-permute-done.refs_0_ = f32[8,2176]{1,0:T(8,128)S(1)} collective-permute-done((f32[8,2176]{1,0:T(8,128)S(1)}, f32[8,2176]{1,0:T(8,128)S(1)}, u32[]{:S(2)}, u32[]{:S(2)}) %collective-permute-start) | collective-permute-done | bytes 69664 | tf_op jit(solution)/shard_map/ppermute | solution.py:459
  16.6 0.1 slice.8
  16.6 0.1 pad_maximum_fusion
  16.7 0.6 broadcast_in_dim.14
  17.4 4.9 %all-to-all-start = ((f32[8,16,128]{2,1,0:T(8,128)}), f32[8,16,128]{2,1,0:T(8,128)S(1)}, u32[]{:S(2)}, u32[]{:S(2)}) async-start(f32[8,16,128]{2,1,0:T(8,128)} %broadcast_in_dim.14), calls=%async_computation | async-start | bytes 131072 | tf_op jit(solution)/shard_map/all_to_all | solution.py:434
  22.3 0.4 shard_map.106
  22.8 1.0 shard_map.107
  23.7 4.8 %all-to-all-done.arrived_ref.refs_0_ = f32[8,16,128]{2,1,0:T(8,128)S(1)} async-done(((f32[8,16,128]{2,1,0:T(8,128)}), f32[8,16,128]{2,1,0:T(8,128)S(1)}, u32[]{:S(2)}, u32[]{:S(2)}) %all-to-all-start) | async-done | bytes 65568 | tf_op jit(solution)/shard_map/all_to_all | solution.py:434
  28.6 1.3 shard_map.105
  29.8 16.7 %shard_map.110 = f32[8,8,8,128]{3,2,1,0:T(8,128)} custom-call(s32[1,1]{1,0:T(1,128)} %get-tuple-element.29.refs_0_, f32[8,8,128]{2,1,0:T(8,128)S(1)} %get-tuple-element.30.refs_1_, bf16[32,4096]{1,0:T(8,128)(2,1)S(1)} %get-tuple-element.22.refs_1_.refs_2_.refs_3_, bf16[80,4096]{1,0:T(8,128)(2,1)S(1)} %get-tuple-element.23.refs_2_.refs_3_.refs_4_, ...), custom_call_target="tpu_custom_call" | custom-call | flops 5033164800 | bytes 2457600 | tf_op jit(solution)/shard_map/pallas_call | solution.py:413
  46.6 3.6 %all-to-all-start.2 = ((f32[8,64,128]{2,1,0:T(8,128)}), f32[8,64,128]{2,1,0:T(8,128)S(1)}, u32[]{:S(2)}, u32[]{:S(2)}) async-start(f32[8,64,128]{2,1,0:T(8,128)} %bitcast.10), calls=%async_computation.2 | async-start | bytes 524288 | tf_op jit(solution)/shard_map/all_to_all | solution.py:434
  50.2 21.1 %shard_map.108 = f32[8,8,8,128]{3,2,1,0:T(8,128)} custom-call(f32[8,16,128]{2,1,0:T(8,128)S(1)} %all-to-all-done.arrived_ref.refs_0_, bf16[32,4096]{1,0:T(8,128)(2,1)S(1)} %get-tuple-element.22.refs_1_.refs_2_.refs_3_, bf16[80,4096]{1,0:T(8,128)(2,1)S(1)} %get-tuple-element.23.refs_2_.refs_3_.refs_4_, ...), custom_call_target="tpu_custom_call" | custom-call | flops 5033164800 | bytes 2457600 | tf_op jit(solution)/shard_map/pallas_call | solution.py:413
  71.3 0.1 copy.12
  71.4 5.4 %all-to-all-start.1 = ((f32[8,64,128]{2,1,0:T(8,128)}), f32[8,64,128]{2,1,0:T(8,128)S(1)}, u32[]{:S(2)}, u32[]{:S(2)}) async-start(f32[8,64,128]{2,1,0:T(8,128)} %bitcast.7), calls=%async_computation.1 | async-start | bytes 524288 | tf_op jit(solution)/shard_map/all_to_all | solution.py:434
  76.8 16.0 %shard_map.111 = (f32[1,8,8,128]{3,2,1,0:T(8,128)S(1)}, f32[8,8,128]{2,1,0:T(8,128)S(1)}) custom-call(s32[1,1]{1,0:T(1,128)} %get-tuple-element.29.refs_0_, f32[8,8,128]{2,1,0:T(8,128)S(1)} %get-tuple-element.30.refs_1_, f32[8,8,8,128]{3,2,1,0:T(8,128)S(1)} %bitcast.27, bf16[32,4096]{1,0:T(8,128)(2,1)S(1)} %get-tuple-element.22.refs_1_.refs_2_.refs_3_, ...), custom_call_target="tpu_custom_call" | custom-call | flops 5033164800 | bytes 2457600 | tf_op jit(solution)/shard_map/pallas_call | solution.py:413
  92.8 20.4 %shard_map.109 = (f32[1,8,8,128]{3,2,1,0:T(8,128)S(1)}, f32[8,8,128]{2,1,0:T(8,128)S(1)}) custom-call(f32[8,16,128]{2,1,0:T(8,128)S(1)} %all-to-all-done.arrived_ref.refs_0_, f32[8,8,8,128]{3,2,1,0:T(8,128)S(1)} %bitcast.26, bf16[32,4096]{1,0:T(8,128)(2,1)S(1)} %get-tuple-element.22.refs_1_.refs_2_.refs_3_, ...), custom_call_target="tpu_custom_call" | custom-call | flops 5033164800 | bytes 2457600 | tf_op jit(solution)/shard_map/pallas_call | solution.py:413
  113.3 1.5 %shard_map.112 = (f32[8,16,128]{2,1,0:T(8,128)}, f32[8,8,128]{2,1,0:T(8,128)S(1)}) custom-call(f32[128,8]{1,0:T(8,128)S(1)} %bitcast.28, f32[8,8,128]{2,1,0:T(8,128)S(1)} %bitcast.31, f32[8,8,128]{2,1,0:T(8,128)S(1)} %bitcast.30, f32[8,8,128]{2,1,0:T(8,128)S(1)} %get-tuple-element.32.table_ref), custom_call_target="tpu_custom_call" | custom-call | tf_op jit(solution)/shard_map/pallas_call | solution.py:221
  114.8 0.6 copy-done.1
  115.4 5.7 %all-to-all-start.3 = ((f32[8,16,128]{2,1,0:T(8,128)}), f32[8,16,128]{2,1,0:T(8,128)S(1)}, u32[]{:S(2)}, u32[]{:S(2)}) async-start(f32[8,16,128]{2,1,0:T(8,128)} %get-tuple-element.33), calls=%async_computation.3 | async-start | bytes 131072 | tf_op jit(solution)/shard_map/all_to_all | solution.py:434
  121.1 6.3 %all-to-all-done.3.sums_ref = f32[8,16,128]{2,1,0:T(8,128)S(1)} async-done(((f32[8,16,128]{2,1,0:T(8,128)}), f32[8,16,128]{2,1,0:T(8,128)S(1)}, u32[]{:S(2)}, u32[]{:S(2)}) %all-to-all-start.3) | async-done | bytes 65568 | tf_op jit(solution)/shard_map/all_to_all | solution.py:434
  127.3 0.6 copy-done.4
  128.0 1.5 %shard_map.113 = (f32[1,1,3,256]{3,2,1,0:T(4,128)}, f32[1,1,3,256]{3,2,1,0:T(4,128)}) custom-call(s32[1]{0:T(128)} %bitcast.member_ref, f32[8,16,128]{2,1,0:T(8,128)} %copy-done.4, f32[8,8,128]{2,1,0:T(8,128)} %copy-done, f32[8,8,128]{2,1,0:T(8,128)} %copy-done.1), custom_call_target="tpu_custom_call" | custom-call | tf_op jit(solution)/shard_map/pallas_call | solution.py:249
  129.4 1.3 copy.13
  130.7 0.6 copy.14
  (28 shorter events, 0.1 us)
Async XLA Ops:
  0.6 0.7 copy-start.11
  0.6 0.8 copy-start.5
  1.4 0.9 copy-start.7
  1.4 0.9 copy-start.8
  2.4 0.7 copy-start.2
  2.4 0.7 copy-start.3
  3.6 5.7 %copy-start.9 = (f32[1,1,3,128]{3,1,2,0:T(1,128)S(1)}, f32[1,1,3,128]{3,1,2,0:T(1,128)}, u32[]{:S(2)}) copy-start(f32[1,1,3,128]{3,1,2,0:T(1,128)} %param.13) | copy-start | bytes 4612
  3.6 5.7 %copy-start.10 = (f32[1,1,3,128]{3,1,2,0:T(1,128)S(1)}, f32[1,1,3,128]{3,1,2,0:T(1,128)}, u32[]{:S(2)}) copy-start(f32[1,1,3,128]{3,1,2,0:T(1,128)} %param.12) | copy-start | bytes 4612
  3.6 7.6 %collective-permute-start.1 = (f32[8,2176]{1,0:T(8,128)S(1)}, f32[8,2176]{1,0:T(8,128)S(1)}, u32[]{:S(2)}, u32[]{:S(2)}) collective-permute-start(f32[8,2176]{1,0:T(8,128)S(1)} %get-tuple-element.20), channel_id=1, source_target_pairs={{8,0},{16,8},{24,16},{32,24},{40,32},{48,40},{56,48},{64,56},{72,6... | collective-permute-start | bytes 208904 | tf_op jit(solution)/shard_map/ppermute | solution.py:460
  9.2 7.3 %collective-permute-start = (f32[8,2176]{1,0:T(8,128)S(1)}, f32[8,2176]{1,0:T(8,128)S(1)}, u32[]{:S(2)}, u32[]{:S(2)}) collective-permute-start(f32[8,2176]{1,0:T(8,128)S(1)} %get-tuple-element.19), channel_id=1, source_target_pairs={{0,8},{8,16},{16,24},{24,32},{32,40},{40,48},{48,56},{56,64},{64,7... | collective-permute-start | bytes 208904 | tf_op jit(solution)/shard_map/ppermute | solution.py:459
  17.4 11.2 %all-to-all-start = ((f32[8,16,128]{2,1,0:T(8,128)}), f32[8,16,128]{2,1,0:T(8,128)S(1)}, u32[]{:S(2)}, u32[]{:S(2)}) async-start(f32[8,16,128]{2,1,0:T(8,128)} %broadcast_in_dim.14), calls=%async_computation | async-start | bytes 131072 | tf_op jit(solution)/shard_map/all_to_all | solution.py:434
  46.6 24.8 %all-to-all-start.2 = ((f32[8,64,128]{2,1,0:T(8,128)}), f32[8,64,128]{2,1,0:T(8,128)S(1)}, u32[]{:S(2)}, u32[]{:S(2)}) async-start(f32[8,64,128]{2,1,0:T(8,128)} %bitcast.10), calls=%async_computation.2 | async-start | bytes 524288 | tf_op jit(solution)/shard_map/all_to_all | solution.py:434
  71.4 21.4 %all-to-all-start.1 = ((f32[8,64,128]{2,1,0:T(8,128)}), f32[8,64,128]{2,1,0:T(8,128)S(1)}, u32[]{:S(2)}, u32[]{:S(2)}) async-start(f32[8,64,128]{2,1,0:T(8,128)} %bitcast.7), calls=%async_computation.1 | async-start | bytes 524288 | tf_op jit(solution)/shard_map/all_to_all | solution.py:434
  113.3 1.5 %copy-start = (f32[8,8,128]{2,1,0:T(8,128)}, f32[8,8,128]{2,1,0:T(8,128)S(1)}, u32[]{:S(2)}) copy-start(f32[8,8,128]{2,1,0:T(8,128)S(1)} %get-tuple-element.34.own_ref) | copy-start | bytes 98308
  114.8 0.6 copy-start.1
  115.4 12.0 %all-to-all-start.3 = ((f32[8,16,128]{2,1,0:T(8,128)}), f32[8,16,128]{2,1,0:T(8,128)S(1)}, u32[]{:S(2)}, u32[]{:S(2)}) async-start(f32[8,16,128]{2,1,0:T(8,128)} %get-tuple-element.33), calls=%async_computation.3 | async-start | bytes 131072 | tf_op jit(solution)/shard_map/all_to_all | solution.py:434
  127.3 0.6 copy-start.4
  129.4 1.3 copy-start.6

commit v3 on v2

--- a/solution.py
+++ b/solution.py
@@ -230,32 +230,8 @@
     )(rank, own, moved, table)
 
 
-def finish_kernel(member_ref, sums_ref, own_ref, slot_ref, pos_ref, vort_ref):
-    member = member_ref[0]
-    total = sums_ref[0]
-    for sender in range(1, sums_ref.shape[0]):
-        total = total + sums_ref[sender]
-    width = own_ref.shape[2]
-    for at, ref in ((0, own_ref), (1, slot_ref)):
-        table = ref[member]
-        result = (table + time_step * total[8 * at : 8 * at + 8]) * table[6:7]
-        lanes = slice(at * width, at * width + width)
-        pos_ref[0, 0, :, lanes] = result[0:3]
-        vort_ref[0, 0, :, lanes] = result[3:6]
-
-
-def finish(member, sums, own, slots):
-    shape = jax.ShapeDtypeStruct((1, 1, 3, 2 * own.shape[2]), f32)
-    return pl.pallas_call(
-        finish_kernel,
-        in_specs=[pl.BlockSpec(memory_space=pltpu.SMEM), whole, whole, whole],
-        out_specs=[whole] * 2,
-        out_shape=[shape, shape],
-    )(member.reshape(1), sums, own, slots)
-
-
 CHUNK = 128
-FINE = 32
+FINE = 16
 SLOTS = 6
 AHEAD = 3
 
@@ -272,9 +248,16 @@
     held = refs[3:]
     halves, rows, half = tgt_ref.shape
 
-    def run():
+    def run(parts):
+        lanes = parts * half
+
         def joined(ref):
-            return jnp.concatenate([ref[0], ref[1]], axis=1)
+            return ref[0] if parts == 1 else jnp.concatenate([ref[0], ref[1]], axis=1)
+
+        def store(ref, values):
+            for part in range(halves):
+                at = slice(part * half, part * half + half)
+                ref[part] = values[:, at] if part < parts else jnp.zeros((rows, half), f32)
 
         table = joined(tgt_ref)
         if moved:
@@ -282,20 +265,19 @@
             for sender in range(1, moved_ref.shape[0]):
                 step = step + joined(moved_ref.at[sender])
             table = table + time_step * step
-            table_ref[0] = table[:, :half]
-            table_ref[1] = table[:, half:]
+            store(table_ref, table)
         where = [(table[k : k + 1, :] - centre) * (1.0 / unit) for k in range(3)]
         vortex = [table[3 + k : 4 + k, :] for k in range(3)]
         square = where[0] * where[0] + where[1] * where[1] + where[2] * where[2]
         square_parts = three_pieces(square)
         tgt[...] = jnp.zeros_like(tgt)
         for k in range(3):
-            parts = three_pieces(-2.0 * where[k])
-            for place, part in enumerate((0, 1, 0, 2, 0, 1)):
-                tgt[3 * place + k : 3 * place + k + 1, :] = parts[part]
-            tgt[18 + k : 19 + k, :] = jnp.ones_like(square)
-            tgt[21 + k : 22 + k, :] = square_parts[k]
-        targets = tgt[...].astype(bf16)
+            pieces = three_pieces(-2.0 * where[k])
+            for place, piece in enumerate((0, 1, 0, 2, 0, 1)):
+                tgt[3 * place + k : 3 * place + k + 1, :lanes] = pieces[piece]
+            tgt[18 + k : 19 + k, :lanes] = jnp.ones_like(square)
+            tgt[21 + k : 22 + k, :lanes] = square_parts[k]
+        targets = tgt[:, :lanes].astype(bf16)
         near_sums[...] = jnp.zeros_like(near_sums)
         grad_sums[...] = jnp.zeros_like(grad_sums)
         start = jnp.minimum(pl.program_id(0), 0)
@@ -307,10 +289,10 @@
             return source_refs[3 * number + which][:, place * CHUNK : (place + 1) * CHUNK]
 
         def read(ref, at, count):
-            return ref[pl.ds(pl.multiple_of(start * CHUNK + at, count), count), :]
+            return ref[pl.ds(pl.multiple_of(start * CHUNK + at, count), count), :lanes]
 
         def distances(chunk):
-            held[chunk % SLOTS][...] = lax.dot_general(
+            held[chunk % SLOTS][:, :lanes] = lax.dot_general(
                 source(2, chunk), targets, (((0,), (0,)), ((), ())), preferred_element_type=f32
             )
 
@@ -328,13 +310,15 @@
                     (grad_ref, fifth * (square_inv + 0.6)),
                 ):
                     high = weight.astype(bf16)
-                    ref[at : at + FINE, :] = high
-                    ref[CHUNK + at : CHUNK + at + FINE, :] = (weight - high.astype(f32)).astype(bf16)
+                    ref[at : at + FINE, :lanes] = high
+                    low = (weight - high.astype(f32)).astype(bf16)
+                    ref[CHUNK + at : CHUNK + at + FINE, :lanes] = low
 
         def sums(chunk):
-            for which, ref, total in ((0, held[SLOTS + chunk % SLOTS], near_sums), (1, held[2 * SLOTS + chunk % SLOTS], grad_sums)):
+            for which, total in ((0, near_sums), (1, grad_sums)):
+                ref = held[(1 + which) * SLOTS + chunk % SLOTS]
                 terms = source(which, chunk)
-                total[...] += dot(
+                total[:, :lanes] += dot(
                     jnp.concatenate([terms, terms], axis=1), read(ref, 0, 2 * CHUNK)
                 )
 
@@ -348,8 +332,8 @@
             weights(chunk)
         for chunk in range(chunks - AHEAD, chunks):
             sums(chunk)
-        near = near_sums[0:8, :] + near_sums[8:16, :] + near_sums[16:24, :]
-        grad = grad_sums[0:24, :] + grad_sums[24:48, :] + grad_sums[48:72, :]
+        near = near_sums[0:8, :lanes] + near_sums[8:16, :lanes] + near_sums[16:24, :lanes]
+        grad = grad_sums[0:24, :lanes] + grad_sums[24:48, :lanes] + grad_sums[48:72, :lanes]
 
         def three(values, first):
             return [values[first + k : first + k + 1, :] for k in range(3)]
@@ -367,19 +351,19 @@
             inner = [inner[k] - vortex[axis] * (turned[k] - outer[k]) for k in range(3)]
         turned = cross(vortex, near_vort)
         stretch = [stretch_factor * (turned[k] - 5.0 * inner[k]) for k in range(3)]
-        blank = jnp.zeros((2, 2 * half), f32)
+        blank = jnp.zeros((2, lanes), f32)
         result = jnp.concatenate(velocity + stretch + [blank], axis=0)
         for copy in range(copies):
-            out_ref[copy, 0] = result[:, :half]
-            out_ref[copy, 1] = result[:, half:]
+            store(out_ref.at[copy], result)
 
     if not counted:
-        run()
+        run(halves)
         return
-    used = pl.program_id(0) * 2 * half < count_ref[0, 0]
-    pl.when(used)(run)
-
-    @pl.when(jnp.logical_not(used))
+    left = count_ref[0, 0] - pl.program_id(0) * halves * half
+    pl.when(left > half)(functools.partial(run, halves))
+    pl.when(jnp.logical_and(left > 0, left <= half))(functools.partial(run, 1))
+
+    @pl.when(left <= 0)
     def _():
         out_ref[...] = jnp.zeros_like(out_ref)
         if moved:
@@ -474,7 +458,19 @@
     second_b, table_b = pair_sums(table_b, sets, 1, moved=moved_b, count=count)
     rank = rank.reshape(2, groups, CAP, groups).transpose(0, 3, 2, 1).reshape(rank.shape)
     sums, table_b = expand_slots(rank, second_a[0], second_b[0], table_b)
-    return finish(lax.axis_index("grp"), swap(sums), table_a, table_b)
+    sums = swap(sums)
+    member = lax.axis_index("grp")
+    own = [lax.dynamic_index_in_dim(t, member, 0, keepdims=False) for t in (table_a, table_b)]
+    total = jnp.sum(sums, axis=0)
+    outs = []
+    for first in (0, 3):
+        moved = [
+            (own[k][first : first + 3] + time_step * total[8 * k + first : 8 * k + first + 3])
+            * own[k][6:7]
+            for k in range(2)
+        ]
+        outs.append(jnp.concatenate(moved, axis=1)[None, None])
+    return tuple(outs)
 
 
 def solution(mesh):

time: 132 us -> 125 us (0.947)
  Pallas kernels: 80.4 us -> 75.6 us
  local copies, waits for them, and re-layouts: 6.36 us -> 4.43 us
    pallas_call x4, Pallas kernels: 74.3 us -> 71 us  [pair_sums(): pl.pallas_call(functools.partial(pairs_kernel, len(source_sets), moved is...]
    pallas_call x2 -> x0, local copies, waits for them, and re-layouts: 1.85 us -> none  [finish(): pl.pallas_call(finish_kernel, in_specs=[pl.BlockSpec(memory_space=pltpu.S...]
    pallas_call x1 -> x0, Pallas kernels: 1.47 us -> none  [finish(): pl.pallas_call(finish_kernel, in_specs=[pl.BlockSpec(memory_space=pltpu.S...]
    unnamed x27 -> x21, local copies, waits for them, and re-layouts: 3.56 us -> 3.47 us
  transfers between devices with their start and end apart: 6 -> 6, of which waited for: 4 -> 4; matrix products, arithmetic and copies ran while one was open for 0% -> 0% of each run, Pallas kernels for 29% -> 30%
where the time goes in v3:
time: 125 us
  Pallas kernels  75.6 us (60%)
  starting transfers between devices  25.3 us (20%)
  waiting for transfers between devices  18.4 us (15%)
  local copies, waits for them, and re-layouts  4.43 us (4%)
    pallas_call x4, Pallas kernels, pair_sums(): pl.pallas_call(functools.partial(pairs_kernel, len(source_sets), moved is...  71 us
    all_to_all x4, starting transfers between devices, swap(): lax.all_to_all(values, 'grp', split_axis=0, concat_axis=0, tiled=True)  19.6 us
    all_to_all x4, waiting for transfers between devices, swap(): lax.all_to_all(values, 'grp', split_axis=0, concat_axis=0, tiled=True)  11.1 us
    ppermute x1, starting transfers between devices, per_device(): lax.ppermute(going_down, 'slab', [((i + 1) % slabs, i) for i in range(sla...  5.64 us
    ppermute x1, waiting for transfers between devices, per_device(): lax.ppermute(going_up, 'slab', [(i, (i + 1) % slabs) for i in range(slabs)])  5.4 us
    unnamed x21, local copies, waits for them, and re-layouts  3.47 us
  transfers between devices with their start and end apart: 6, of which 4 were waited for; matrix products, arithmetic and copies ran while one was open for 0% of the time, Pallas kernels for 30%

profile of v3, /device:TPU:0, one launch (start us, length us, event | category | flops | bytes accessed | tf_op | source)
XLA Modules:
  0.0 124.6 jit_solution(14030100189427029675)
XLA Ops:
  0.6 0.6 copy-done.7
  1.3 0.1 copy.11.route_ref
  1.4 0.1 copy-done.2
  1.4 0.9 copy_bitcast_fusion
  2.4 0.0 copy-start
  2.4 0.0 copy-start.1
  2.4 0.7 copy-done
  3.1 0.5 shard_map.104
  3.6 5.6 %collective-permute-start.1 = (f32[8,2176]{1,0:T(8,128)S(1)}, f32[8,2176]{1,0:T(8,128)S(1)}, u32[]{:S(2)}, u32[]{:S(2)}) collective-permute-start(f32[8,2176]{1,0:T(8,128)S(1)} %get-tuple-element.20), channel_id=1, source_target_pairs={{8,0},{16,8},{24,16},{32,24},{40,32},{48,40},{56,48},{64,56},{72,6... | collective-permute-start | bytes 208904 | tf_op jit(solution)/shard_map/ppermute | solution.py:444
  9.2 0.0 collective-permute-start
  9.2 1.9 %collective-permute-done.1.refs_1_ = f32[8,2176]{1,0:T(8,128)S(1)} collective-permute-done((f32[8,2176]{1,0:T(8,128)S(1)}, f32[8,2176]{1,0:T(8,128)S(1)}, u32[]{:S(2)}, u32[]{:S(2)}) %collective-permute-start.1) | collective-permute-done | bytes 69664 | tf_op jit(solution)/shard_map/ppermute | solution.py:444
  11.2 5.4 %collective-permute-done.refs_0_ = f32[8,2176]{1,0:T(8,128)S(1)} collective-permute-done((f32[8,2176]{1,0:T(8,128)S(1)}, f32[8,2176]{1,0:T(8,128)S(1)}, u32[]{:S(2)}, u32[]{:S(2)}) %collective-permute-start) | collective-permute-done | bytes 69664 | tf_op jit(solution)/shard_map/ppermute | solution.py:443
  16.6 0.1 slice.68
  16.6 0.1 pad_maximum_fusion
  16.7 0.6 broadcast_in_dim.20
  17.4 4.9 %all-to-all-start = ((f32[8,16,128]{2,1,0:T(8,128)}), f32[8,16,128]{2,1,0:T(8,128)S(1)}, u32[]{:S(2)}, u32[]{:S(2)}) async-start(f32[8,16,128]{2,1,0:T(8,128)} %broadcast_in_dim.20), calls=%async_computation | async-start | bytes 131072 | tf_op jit(solution)/shard_map/all_to_all | solution.py:418
  22.3 0.4 shard_map.105
  22.8 1.0 shard_map.106
  23.7 4.8 %all-to-all-done.refs_0_.arrived_ref = f32[8,16,128]{2,1,0:T(8,128)S(1)} async-done(((f32[8,16,128]{2,1,0:T(8,128)}), f32[8,16,128]{2,1,0:T(8,128)S(1)}, u32[]{:S(2)}, u32[]{:S(2)}) %all-to-all-start) | async-done | bytes 65568 | tf_op jit(solution)/shard_map/all_to_all | solution.py:418
  28.6 1.3 %shard_map.109 = (f32[8,8,128]{2,1,0:T(8,128)S(1)}, f32[128,8]{1,0:T(8,128)S(1)}, s32[1,1]{1,0:T(1,128)}) custom-call(f32[8,16,128]{2,1,0:T(8,128)S(1)} %all-to-all-done.refs_0_.arrived_ref), custom_call_target="tpu_custom_call" | custom-call | tf_op jit(solution)/shard_map/pallas_call | solution.py:188
  29.8 15.3 %shard_map.110 = f32[8,8,8,128]{3,2,1,0:T(8,128)} custom-call(s32[1,1]{1,0:T(1,128)} %get-tuple-element.30.refs_0_, f32[8,8,128]{2,1,0:T(8,128)S(1)} %get-tuple-element.31.refs_1_, bf16[32,4096]{1,0:T(8,128)(2,1)S(1)} %get-tuple-element.21.refs_1_.refs_2_.refs_3_, bf16[80,4096]{1,0:T(8,128)(2,1)S(1)} %get-tuple-element.22.refs_2_.refs_3_.refs_4_, ...), custom_call_target="tpu_custom_call" | custom-call | flops 5033164800 | bytes 2457600 | tf_op jit(solution)/shard_map/pallas_call | solution.py:397
  45.1 3.6 %all-to-all-start.2 = ((f32[8,64,128]{2,1,0:T(8,128)}), f32[8,64,128]{2,1,0:T(8,128)S(1)}, u32[]{:S(2)}, u32[]{:S(2)}) async-start(f32[8,64,128]{2,1,0:T(8,128)} %bitcast.10), calls=%async_computation.2 | async-start | bytes 524288 | tf_op jit(solution)/shard_map/all_to_all | solution.py:418
  48.7 20.8 %shard_map.107 = f32[8,8,8,128]{3,2,1,0:T(8,128)} custom-call(f32[8,16,128]{2,1,0:T(8,128)S(1)} %all-to-all-done.refs_0_.arrived_ref, bf16[32,4096]{1,0:T(8,128)(2,1)S(1)} %get-tuple-element.21.refs_1_.refs_2_.refs_3_, bf16[80,4096]{1,0:T(8,128)(2,1)S(1)} %get-tuple-element.22.refs_2_.refs_3_.refs_4_, ...), custom_call_target="tpu_custom_call" | custom-call | flops 5033164800 | bytes 2457600 | tf_op jit(solution)/shard_map/pallas_call | solution.py:397
  69.5 0.1 copy.12
  69.6 5.4 %all-to-all-start.1 = ((f32[8,64,128]{2,1,0:T(8,128)}), f32[8,64,128]{2,1,0:T(8,128)S(1)}, u32[]{:S(2)}, u32[]{:S(2)}) async-start(f32[8,64,128]{2,1,0:T(8,128)} %bitcast.3), calls=%async_computation.1 | async-start | bytes 524288 | tf_op jit(solution)/shard_map/all_to_all | solution.py:418
  75.0 14.6 %shard_map.111 = (f32[1,8,8,128]{3,2,1,0:T(8,128)S(1)}, f32[8,8,128]{2,1,0:T(8,128)S(1)}) custom-call(s32[1,1]{1,0:T(1,128)} %get-tuple-element.30.refs_0_, f32[8,8,128]{2,1,0:T(8,128)S(1)} %get-tuple-element.31.refs_1_, f32[8,8,8,128]{3,2,1,0:T(8,128)S(1)} %bitcast.42, bf16[32,4096]{1,0:T(8,128)(2,1)S(1)} %get-tuple-element.21.refs_1_.refs_2_.refs_3_, ...), custom_call_target="tpu_custom_call" | custom-call | flops 5033164800 | bytes 2457600 | tf_op jit(solution)/shard_map/pallas_call | solution.py:397
  89.6 20.4 %shard_map.108 = (f32[1,8,8,128]{3,2,1,0:T(8,128)S(1)}, f32[8,8,128]{2,1,0:T(8,128)S(1)}) custom-call(f32[8,16,128]{2,1,0:T(8,128)S(1)} %all-to-all-done.refs_0_.arrived_ref, f32[8,8,8,128]{3,2,1,0:T(8,128)S(1)} %bitcast.41, bf16[32,4096]{1,0:T(8,128)(2,1)S(1)} %get-tuple-element.21.refs_1_.refs_2_.refs_3_, ...), custom_call_target="tpu_custom_call" | custom-call | flops 5033164800 | bytes 2457600 | tf_op jit(solution)/shard_map/pallas_call | solution.py:397
  110.0 1.5 %shard_map.112 = (f32[8,16,128]{2,1,0:T(8,128)}, f32[8,8,128]{2,1,0:T(8,128)S(1)}) custom-call(f32[128,8]{1,0:T(8,128)S(1)} %bitcast.43, f32[8,8,128]{2,1,0:T(8,128)S(1)} %bitcast.46, f32[8,8,128]{2,1,0:T(8,128)S(1)} %bitcast.45, f32[8,8,128]{2,1,0:T(8,128)S(1)} %get-tuple-element.33.table_ref), custom_call_target="tpu_custom_call" | custom-call | tf_op jit(solution)/shard_map/pallas_call | solution.py:221
  111.5 5.7 %all-to-all-start.3 = ((f32[8,16,128]{2,1,0:T(8,128)}), f32[8,16,128]{2,1,0:T(8,128)S(1)}, u32[]{:S(2)}, u32[]{:S(2)}) async-start(f32[8,16,128]{2,1,0:T(8,128)} %get-tuple-element.34), calls=%async_computation.3 | async-start | bytes 131072 | tf_op jit(solution)/shard_map/all_to_all | solution.py:418
  117.2 6.2 %all-to-all-done.3 = f32[8,16,128]{2,1,0:T(8,128)S(1)} async-done(((f32[8,16,128]{2,1,0:T(8,128)}), f32[8,16,128]{2,1,0:T(8,128)S(1)}, u32[]{:S(2)}, u32[]{:S(2)}) %all-to-all-start.3) | async-done | bytes 65568 | tf_op jit(solution)/shard_map/all_to_all | solution.py:418
  123.5 0.6 copy.13
  124.0 0.6 copy.14
  (27 shorter events, 0.1 us)
Async XLA Ops:
  0.6 0.7 copy-start.7
  0.6 0.8 copy-start.2
  1.4 0.9 copy-start.3
  1.4 0.9 copy-start.4
  2.4 0.7 copy-start
  2.4 0.7 copy-start.1
  3.6 5.7 %copy-start.5 = (f32[1,1,3,128]{3,1,2,0:T(1,128)S(1)}, f32[1,1,3,128]{3,1,2,0:T(1,128)}, u32[]{:S(2)}) copy-start(f32[1,1,3,128]{3,1,2,0:T(1,128)} %param.13) | copy-start | bytes 4612
  3.6 5.7 %copy-start.6 = (f32[1,1,3,128]{3,1,2,0:T(1,128)S(1)}, f32[1,1,3,128]{3,1,2,0:T(1,128)}, u32[]{:S(2)}) copy-start(f32[1,1,3,128]{3,1,2,0:T(1,128)} %param.12) | copy-start | bytes 4612
  3.6 7.6 %collective-permute-start.1 = (f32[8,2176]{1,0:T(8,128)S(1)}, f32[8,2176]{1,0:T(8,128)S(1)}, u32[]{:S(2)}, u32[]{:S(2)}) collective-permute-start(f32[8,2176]{1,0:T(8,128)S(1)} %get-tuple-element.20), channel_id=1, source_target_pairs={{8,0},{16,8},{24,16},{32,24},{40,32},{48,40},{56,48},{64,56},{72,6... | collective-permute-start | bytes 208904 | tf_op jit(solution)/shard_map/ppermute | solution.py:444
  9.2 7.3 %collective-permute-start = (f32[8,2176]{1,0:T(8,128)S(1)}, f32[8,2176]{1,0:T(8,128)S(1)}, u32[]{:S(2)}, u32[]{:S(2)}) collective-permute-start(f32[8,2176]{1,0:T(8,128)S(1)} %get-tuple-element.19), channel_id=1, source_target_pairs={{0,8},{8,16},{16,24},{24,32},{32,40},{40,48},{48,56},{56,64},{64,7... | collective-permute-start | bytes 208904 | tf_op jit(solution)/shard_map/ppermute | solution.py:443
  17.4 11.2 %all-to-all-start = ((f32[8,16,128]{2,1,0:T(8,128)}), f32[8,16,128]{2,1,0:T(8,128)S(1)}, u32[]{:S(2)}, u32[]{:S(2)}) async-start(f32[8,16,128]{2,1,0:T(8,128)} %broadcast_in_dim.20), calls=%async_computation | async-start | bytes 131072 | tf_op jit(solution)/shard_map/all_to_all | solution.py:418
  45.1 24.5 %all-to-all-start.2 = ((f32[8,64,128]{2,1,0:T(8,128)}), f32[8,64,128]{2,1,0:T(8,128)S(1)}, u32[]{:S(2)}, u32[]{:S(2)}) async-start(f32[8,64,128]{2,1,0:T(8,128)} %bitcast.10), calls=%async_computation.2 | async-start | bytes 524288 | tf_op jit(solution)/shard_map/all_to_all | solution.py:418
  69.6 20.0 %all-to-all-start.1 = ((f32[8,64,128]{2,1,0:T(8,128)}), f32[8,64,128]{2,1,0:T(8,128)S(1)}, u32[]{:S(2)}, u32[]{:S(2)}) async-start(f32[8,64,128]{2,1,0:T(8,128)} %bitcast.3), calls=%async_computation.1 | async-start | bytes 524288 | tf_op jit(solution)/shard_map/all_to_all | solution.py:418
  111.5 11.9 %all-to-all-start.3 = ((f32[8,16,128]{2,1,0:T(8,128)}), f32[8,16,128]{2,1,0:T(8,128)S(1)}, u32[]{:S(2)}, u32[]{:S(2)}) async-start(f32[8,16,128]{2,1,0:T(8,128)} %get-tuple-element.34), calls=%async_computation.3 | async-start | bytes 131072 | tf_op jit(solution)/shard_map/all_to_all | solution.py:418

commit v4 on v3

--- a/solution.py
+++ b/solution.py
@@ -53,7 +53,7 @@
     faces, pos_ref, vort_ref, valid_ref, mig_pos_ref, mig_vort_ref, mig_valid_ref, route_ref,
     up_ref, down_ref, record,
 ):
-    sources = pos_ref.shape[1]
+    sources = pos_ref.shape[2]
     migrants = route_ref.shape[0]
     slots = (up_ref.shape[1] - faces) // 2
     destinations = 2 * slots // CAP
@@ -68,8 +68,9 @@
     placing = (route * CAP + order) == lax.broadcasted_iota(jnp.int32, (migrants, 2 * slots), 1)
     placing = jnp.where(placing, 1.0, 0.0).astype(bf16)
     record[...] = jnp.zeros_like(record)
-    record[0:3, :] = mig_pos_ref[...]
-    record[3:6, :] = mig_vort_ref[...]
+    for k in range(3):
+        record[k : k + 1, :] = mig_pos_ref[k]
+        record[3 + k : 4 + k, :] = mig_vort_ref[k]
     record[6:7, :] = mig_valid_ref[...].astype(f32)
     pieces = jnp.concatenate(three_pieces(record[...]), axis=0)
     placed = dot(jnp.concatenate([pieces, jnp.zeros((8, migrants), f32)], axis=0).astype(bf16), placing)
@@ -78,9 +79,10 @@
     for ref, begin, shift, which in ((down_ref, 0, 1.0, 0), (up_ref, sources - faces, -1.0, 1)):
         piece = slice(begin, begin + faces)
         mask = valid_ref[which : which + 1, :].astype(f32)
-        ref[0:1, :faces] = pos_ref[0:1, piece] + shift
-        ref[1:3, :faces] = pos_ref[1:3, piece]
-        ref[3:6, :faces] = vort_ref[:, piece] * mask
+        for k in range(3):
+            place = pos_ref[k, :, piece]
+            ref[k : k + 1, :faces] = place + shift if k == 0 else place
+            ref[3 + k : 4 + k, :faces] = vort_ref[k, :, piece] * mask
         ref[6:8, :faces] = jnp.zeros((2, faces), f32)
         ref[:, faces:] = jnp.where(first, placed + shift, placed)
 
@@ -104,7 +106,7 @@
 
     def columns(row):
         if source_refs[0].shape[0] == 3:
-            return source_refs[row // 3][row % 3 : row % 3 + 1, :]
+            return source_refs[row // 3][row % 3]
         return jnp.concatenate([ref[row : row + 1, : length // 2] for ref in source_refs], axis=1)
 
     places = [(columns(k) - centre) * (1.0 / unit) for k in range(3)]
@@ -204,12 +206,10 @@
         jnp.concatenate([ref[m] for m in range(groups)], axis=1) for ref in (moved_ref, table_ref)
     ]
     pieces = jnp.concatenate(three_pieces(jnp.concatenate(rows, axis=0)), axis=0).astype(bf16)
-    wanted = lax.broadcasted_iota(jnp.int32, (slots, groups * slots), 1).astype(f32)
+    wanted = lax.broadcasted_iota(jnp.int32, (groups * slots, slots), 0).astype(f32)
     for member in range(groups):
-        chosen = jnp.where(rank_ref[:, member : member + 1] == wanted, 1.0, 0.0).astype(bf16)
-        found = lax.dot_general(
-            pieces, chosen, (((1,), (1,)), ((), ())), preferred_element_type=f32
-        )
+        chosen = jnp.where(rank_ref[member : member + 1, :] == wanted, 1.0, 0.0).astype(bf16)
+        found = dot(pieces, chosen)
         found = found[0:16] + found[16:32] + found[32:48]
         sums_ref[member, 0:8, :] = own_ref[member]
         sums_ref[member, 8:16, :] = found[0:8]
@@ -427,9 +427,13 @@
 ):
     groups = lax.axis_size("grp")
     slabs = lax.axis_size("slab")
-    places = src_pos[0, 0]
-    vortex = src_vort[0, 0]
-    sources = places.shape[1]
+
+    def components(values):
+        return values.transpose(0, 2, 1, 3)[0]
+
+    places = components(src_pos)
+    vortex = components(src_vort)
+    sources = places.shape[2]
     faces = face_valid.shape[3]
     own = tgt_pos.shape[3]
     slots = groups * CAP
@@ -437,7 +441,7 @@
         [tgt_pos[0, 0], tgt_vort[0, 0], jnp.ones((1, own), f32), jnp.zeros((1, own), f32)], axis=0
     )
     going_up, going_down = make_sends(
-        places, vortex, face_valid[0, 0], mig_pos[0, 0], mig_vort[0, 0], mig_valid[0], mig_route[0, 0],
+        places, vortex, face_valid[0, 0], components(mig_pos), components(mig_vort), mig_valid[0], mig_route[0, 0],
         2 * groups,
     )
     from_lower = lax.ppermute(going_up, "slab", [(i, (i + 1) % slabs) for i in range(slabs)])
@@ -456,7 +460,7 @@
     moved_b = swap(first_b.reshape(groups, -1, 128)).reshape(first_b.shape)
     second_a, table_a = pair_sums(received, sets, 1, moved=moved_a)
     second_b, table_b = pair_sums(table_b, sets, 1, moved=moved_b, count=count)
-    rank = rank.reshape(2, groups, CAP, groups).transpose(0, 3, 2, 1).reshape(rank.shape)
+    rank = rank.reshape(2, groups, CAP, groups).transpose(1, 0, 3, 2).reshape(groups, 2 * slots)
     sums, table_b = expand_slots(rank, second_a[0], second_b[0], table_b)
     sums = swap(sums)
     member = lax.axis_index("grp")
@@ -469,7 +473,8 @@
             * own[k][6:7]
             for k in range(2)
         ]
-        outs.append(jnp.concatenate(moved, axis=1)[None, None])
+        moved = jnp.concatenate([part[:, None, :] for part in moved], axis=2)
+        outs.append(moved[None].transpose(0, 2, 1, 3))
     return tuple(outs)
 
 

time: 125 us -> 127 us (1.016)
  Pallas kernels: 75.6 us -> 77 us
    pallas_call x4, Pallas kernels: 71 us -> 72.7 us  [pair_sums(): pl.pallas_call(functools.partial(pairs_kernel, len(source_sets), moved is...]
    unnamed x21 -> x23, local copies, waits for them, and re-layouts: 3.47 us -> 4.02 us
where the time goes in v4:
time: 127 us
  Pallas kernels  77 us (61%)
  starting transfers between devices  25.4 us (20%)
  waiting for transfers between devices  18.4 us (14%)
  local copies, waits for them, and re-layouts  5.05 us (4%)
    pallas_call x4, Pallas kernels, pair_sums(): pl.pallas_call(functools.partial(pairs_kernel, len(source_sets), moved is...  72.7 us
    all_to_all x4, starting transfers between devices, swap(): lax.all_to_all(values, 'grp', split_axis=0, concat_axis=0, tiled=True)  19.8 us
    all_to_all x4, waiting for transfers between devices, swap(): lax.all_to_all(values, 'grp', split_axis=0, concat_axis=0, tiled=True)  11 us
    ppermute x1, starting transfers between devices, per_device(): lax.ppermute(going_down, 'slab', [((i + 1) % slabs, i) for i in range(sla...  5.64 us
    ppermute x1, waiting for transfers between devices, per_device(): lax.ppermute(going_up, 'slab', [(i, (i + 1) % slabs) for i in range(slabs)])  5.4 us
    unnamed x23, local copies, waits for them, and re-layouts  4.02 us
  transfers between devices with their start and end apart: 6, of which 4 were waited for; matrix products, arithmetic and copies ran while one was open for 0% of the time, Pallas kernels for 30%

profile of v4, /device:TPU:0, one launch (start us, length us, event | category | flops | bytes accessed | tf_op | source)
XLA Modules:
  0.0 126.7 jit_solution(11006965635453247594)
XLA Ops:
  0.6 0.6 copy-done.9
  1.3 0.1 copy.11.route_ref
  1.4 0.0 copy-done
  1.4 0.6 copy-done.4
  2.1 0.0 copy-done.5
  2.1 0.8 copy-done.1
  2.9 0.7 copy-done.3
  3.6 0.5 shard_map.104
  4.1 5.6 %collective-permute-start.1 = (f32[8,2176]{1,0:T(8,128)S(1)}, f32[8,2176]{1,0:T(8,128)S(1)}, u32[]{:S(2)}, u32[]{:S(2)}) collective-permute-start(f32[8,2176]{1,0:T(8,128)S(1)} %get-tuple-element.20), channel_id=1, source_target_pairs={{8,0},{16,8},{24,16},{32,24},{40,32},{48,40},{56,48},{64,56},{72,6... | collective-permute-start | bytes 208904 | tf_op jit(solution)/shard_map/ppermute | solution.py:448
  9.8 1.9 %collective-permute-done.1.refs_1_ = f32[8,2176]{1,0:T(8,128)S(1)} collective-permute-done((f32[8,2176]{1,0:T(8,128)S(1)}, f32[8,2176]{1,0:T(8,128)S(1)}, u32[]{:S(2)}, u32[]{:S(2)}) %collective-permute-start.1) | collective-permute-done | bytes 69664 | tf_op jit(solution)/shard_map/ppermute | solution.py:448
  11.7 5.4 %collective-permute-done.refs_0_ = f32[8,2176]{1,0:T(8,128)S(1)} collective-permute-done((f32[8,2176]{1,0:T(8,128)S(1)}, f32[8,2176]{1,0:T(8,128)S(1)}, u32[]{:S(2)}, u32[]{:S(2)}) %collective-permute-start) | collective-permute-done | bytes 69664 | tf_op jit(solution)/shard_map/ppermute | solution.py:447
  17.1 0.1 slice.68
  17.2 0.1 pad_maximum_fusion
  17.3 0.6 broadcast_in_dim.26
  17.9 5.1 %all-to-all-start = ((f32[8,16,128]{2,1,0:T(8,128)}), f32[8,16,128]{2,1,0:T(8,128)S(1)}, u32[]{:S(2)}, u32[]{:S(2)}) async-start(f32[8,16,128]{2,1,0:T(8,128)} %broadcast_in_dim.26), calls=%async_computation | async-start | bytes 131072 | tf_op jit(solution)/shard_map/all_to_all | solution.py:418
  23.0 0.4 shard_map.105
  23.4 1.0 shard_map.106
  24.4 4.8 %all-to-all-done.refs_0_.arrived_ref = f32[8,16,128]{2,1,0:T(8,128)S(1)} async-done(((f32[8,16,128]{2,1,0:T(8,128)}), f32[8,16,128]{2,1,0:T(8,128)S(1)}, u32[]{:S(2)}, u32[]{:S(2)}) %all-to-all-start) | async-done | bytes 65568 | tf_op jit(solution)/shard_map/all_to_all | solution.py:418
  29.2 1.3 %shard_map.109 = (f32[8,8,128]{2,1,0:T(8,128)S(1)}, f32[128,8]{1,0:T(8,128)S(1)}, s32[1,1]{1,0:T(1,128)}) custom-call(f32[8,16,128]{2,1,0:T(8,128)S(1)} %all-to-all-done.refs_0_.arrived_ref), custom_call_target="tpu_custom_call" | custom-call | tf_op jit(solution)/shard_map/pallas_call | solution.py:190
  30.5 15.6 %shard_map.110 = f32[8,8,8,128]{3,2,1,0:T(8,128)} custom-call(s32[1,1]{1,0:T(1,128)} %get-tuple-element.30.refs_0_, f32[8,8,128]{2,1,0:T(8,128)S(1)} %get-tuple-element.31.refs_1_, bf16[32,4096]{1,0:T(8,128)(2,1)S(1)} %get-tuple-element.21.refs_1_.refs_2_.refs_3_, bf16[80,4096]{1,0:T(8,128)(2,1)S(1)} %get-tuple-element.22.refs_2_.refs_3_.refs_4_, ...), custom_call_target="tpu_custom_call" | custom-call | flops 5033164800 | bytes 2457600 | tf_op jit(solution)/shard_map/pallas_call | solution.py:397
  46.1 3.6 %all-to-all-start.2 = ((f32[8,64,128]{2,1,0:T(8,128)}), f32[8,64,128]{2,1,0:T(8,128)S(1)}, u32[]{:S(2)}, u32[]{:S(2)}) async-start(f32[8,64,128]{2,1,0:T(8,128)} %bitcast.13), calls=%async_computation.2 | async-start | bytes 524288 | tf_op jit(solution)/shard_map/all_to_all | solution.py:418
  49.7 21.3 %shard_map.107 = f32[8,8,8,128]{3,2,1,0:T(8,128)} custom-call(f32[8,16,128]{2,1,0:T(8,128)S(1)} %all-to-all-done.refs_0_.arrived_ref, bf16[32,4096]{1,0:T(8,128)(2,1)S(1)} %get-tuple-element.21.refs_1_.refs_2_.refs_3_, bf16[80,4096]{1,0:T(8,128)(2,1)S(1)} %get-tuple-element.22.refs_2_.refs_3_.refs_4_, ...), custom_call_target="tpu_custom_call" | custom-call | flops 5033164800 | bytes 2457600 | tf_op jit(solution)/shard_map/pallas_call | solution.py:397
  71.0 0.1 copy.12
  71.1 0.1 reshape.34.rank_ref
  71.2 5.4 %all-to-all-start.1 = ((f32[8,64,128]{2,1,0:T(8,128)}), f32[8,64,128]{2,1,0:T(8,128)S(1)}, u32[]{:S(2)}, u32[]{:S(2)}) async-start(f32[8,64,128]{2,1,0:T(8,128)} %bitcast.7), calls=%async_computation.1 | async-start | bytes 524288 | tf_op jit(solution)/shard_map/all_to_all | solution.py:418
  76.6 15.0 %shard_map.111 = (f32[1,8,8,128]{3,2,1,0:T(8,128)S(1)}, f32[8,8,128]{2,1,0:T(8,128)S(1)}) custom-call(s32[1,1]{1,0:T(1,128)} %get-tuple-element.30.refs_0_, f32[8,8,128]{2,1,0:T(8,128)S(1)} %get-tuple-element.31.refs_1_, f32[8,8,8,128]{3,2,1,0:T(8,128)S(1)} %bitcast.45, bf16[32,4096]{1,0:T(8,128)(2,1)S(1)} %get-tuple-element.21.refs_1_.refs_2_.refs_3_, ...), custom_call_target="tpu_custom_call" | custom-call | flops 5033164800 | bytes 2457600 | tf_op jit(solution)/shard_map/pallas_call | solution.py:397
  91.6 20.9 %shard_map.108 = (f32[1,8,8,128]{3,2,1,0:T(8,128)S(1)}, f32[8,8,128]{2,1,0:T(8,128)S(1)}) custom-call(f32[8,16,128]{2,1,0:T(8,128)S(1)} %all-to-all-done.refs_0_.arrived_ref, f32[8,8,8,128]{3,2,1,0:T(8,128)S(1)} %bitcast.46, bf16[32,4096]{1,0:T(8,128)(2,1)S(1)} %get-tuple-element.21.refs_1_.refs_2_.refs_3_, ...), custom_call_target="tpu_custom_call" | custom-call | flops 5033164800 | bytes 2457600 | tf_op jit(solution)/shard_map/pallas_call | solution.py:397
  112.5 1.1 shard_map.112
  113.5 5.7 %all-to-all-start.3 = ((f32[8,16,128]{2,1,0:T(8,128)}), f32[8,16,128]{2,1,0:T(8,128)S(1)}, u32[]{:S(2)}, u32[]{:S(2)}) async-start(f32[8,16,128]{2,1,0:T(8,128)} %get-tuple-element.34), calls=%async_computation.3 | async-start | bytes 131072 | tf_op jit(solution)/shard_map/all_to_all | solution.py:418
  119.3 6.2 %all-to-all-done.3 = f32[8,16,128]{2,1,0:T(8,128)S(1)} async-done(((f32[8,16,128]{2,1,0:T(8,128)}), f32[8,16,128]{2,1,0:T(8,128)S(1)}, u32[]{:S(2)}, u32[]{:S(2)}) %all-to-all-start.3) | async-done | bytes 65568 | tf_op jit(solution)/shard_map/all_to_all | solution.py:418
  125.5 0.6 copy.13
  126.1 0.6 copy.14
  (30 shorter events, 0.1 us)
Async XLA Ops:
  0.6 0.7 copy-start.9
  0.6 0.8 copy-start
  1.4 0.7 copy-start.4
  1.4 0.7 copy-start.5
  1.4 0.7 copy-start.6
  2.1 0.8 copy-start.1
  2.9 0.7 copy-start.3
  4.1 5.7 %copy-start.7 = (f32[1,1,3,128]{3,1,2,0:T(1,128)S(1)}, f32[1,1,3,128]{3,1,2,0:T(1,128)}, u32[]{:S(2)}) copy-start(f32[1,1,3,128]{3,1,2,0:T(1,128)} %param.13) | copy-start | bytes 4612
  4.1 5.7 %copy-start.8 = (f32[1,1,3,128]{3,1,2,0:T(1,128)S(1)}, f32[1,1,3,128]{3,1,2,0:T(1,128)}, u32[]{:S(2)}) copy-start(f32[1,1,3,128]{3,1,2,0:T(1,128)} %param.12) | copy-start | bytes 4612
  4.1 7.6 %collective-permute-start.1 = (f32[8,2176]{1,0:T(8,128)S(1)}, f32[8,2176]{1,0:T(8,128)S(1)}, u32[]{:S(2)}, u32[]{:S(2)}) collective-permute-start(f32[8,2176]{1,0:T(8,128)S(1)} %get-tuple-element.20), channel_id=1, source_target_pairs={{8,0},{16,8},{24,16},{32,24},{40,32},{48,40},{56,48},{64,56},{72,6... | collective-permute-start | bytes 208904 | tf_op jit(solution)/shard_map/ppermute | solution.py:448
  9.7 7.3 %collective-permute-start = (f32[8,2176]{1,0:T(8,128)S(1)}, f32[8,2176]{1,0:T(8,128)S(1)}, u32[]{:S(2)}, u32[]{:S(2)}) collective-permute-start(f32[8,2176]{1,0:T(8,128)S(1)} %get-tuple-element.19), channel_id=1, source_target_pairs={{0,8},{8,16},{16,24},{24,32},{32,40},{40,48},{48,56},{56,64},{64,7... | collective-permute-start | bytes 208904 | tf_op jit(solution)/shard_map/ppermute | solution.py:447
  17.9 5.1 %copy-start.2 = (f32[1,1,3,4096]{3,1,2,0:T(1,128)S(1)}, f32[1,1,3,4096]{3,1,2,0:T(1,128)}, u32[]{:S(2)}) copy-start(f32[1,1,3,4096]{3,1,2,0:T(1,128)} %param.10) | copy-start | bytes 147460
  17.9 11.3 %all-to-all-start = ((f32[8,16,128]{2,1,0:T(8,128)}), f32[8,16,128]{2,1,0:T(8,128)S(1)}, u32[]{:S(2)}, u32[]{:S(2)}) async-start(f32[8,16,128]{2,1,0:T(8,128)} %broadcast_in_dim.26), calls=%async_computation | async-start | bytes 131072 | tf_op jit(solution)/shard_map/all_to_all | solution.py:418
  46.1 25.1 %all-to-all-start.2 = ((f32[8,64,128]{2,1,0:T(8,128)}), f32[8,64,128]{2,1,0:T(8,128)S(1)}, u32[]{:S(2)}, u32[]{:S(2)}) async-start(f32[8,64,128]{2,1,0:T(8,128)} %bitcast.13), calls=%async_computation.2 | async-start | bytes 524288 | tf_op jit(solution)/shard_map/all_to_all | solution.py:418
  71.2 20.4 %all-to-all-start.1 = ((f32[8,64,128]{2,1,0:T(8,128)}), f32[8,64,128]{2,1,0:T(8,128)S(1)}, u32[]{:S(2)}, u32[]{:S(2)}) async-start(f32[8,64,128]{2,1,0:T(8,128)} %bitcast.7), calls=%async_computation.1 | async-start | bytes 524288 | tf_op jit(solution)/shard_map/all_to_all | solution.py:418
  113.5 12.0 %all-to-all-start.3 = ((f32[8,16,128]{2,1,0:T(8,128)}), f32[8,16,128]{2,1,0:T(8,128)S(1)}, u32[]{:S(2)}, u32[]{:S(2)}) async-start(f32[8,16,128]{2,1,0:T(8,128)} %get-tuple-element.34), calls=%async_computation.3 | async-start | bytes 131072 | tf_op jit(solution)/shard_map/all_to_all | solution.py:418

commit v5 on v4

--- a/solution.py
+++ b/solution.py
@@ -96,7 +96,7 @@
         out_specs=[whole] * 2,
         out_shape=[shape, shape],
         scratch_shapes=[pltpu.VMEM((8, route.shape[0]), f32)],
-        compiler_params=pltpu.CompilerParams(vmem_limit_bytes=48 << 20),
+        compiler_params=pltpu.CompilerParams(vmem_limit_bytes=62 << 20),
     )(places, vortex, valid, mig_pos, mig_vort, mig_valid, route)
 
 

time: 127 us -> 127 us (level)
  local copies, waits for them, and re-layouts: 5.05 us -> 3.47 us
  Pallas kernels: 77 us -> 78.5 us
    unnamed x23 -> x13, local copies, waits for them, and re-layouts: 4.02 us -> 1.83 us
    pallas_call x1, Pallas kernels: 0.47 us -> 2.05 us  [make_sends(): pl.pallas_call(functools.partial(send_kernel, faces), in_specs=[whole] *...]
where the time goes in v5:
time: 127 us
  Pallas kernels  78.5 us (62%)
  starting transfers between devices  25.4 us (20%)
  waiting for transfers between devices  18.6 us (15%)
  local copies, waits for them, and re-layouts  3.47 us (3%)
    pallas_call x4, Pallas kernels, pair_sums(): pl.pallas_call(functools.partial(pairs_kernel, len(source_sets), moved is...  72.7 us
    all_to_all x4, starting transfers between devices, swap(): lax.all_to_all(values, 'grp', split_axis=0, concat_axis=0, tiled=True)  19.8 us
    all_to_all x4, waiting for transfers between devices, swap(): lax.all_to_all(values, 'grp', split_axis=0, concat_axis=0, tiled=True)  11 us
    ppermute x1, starting transfers between devices, per_device(): lax.ppermute(going_down, 'slab', [((i + 1) % slabs, i) for i in range(sla...  5.64 us
    ppermute x1, waiting for transfers between devices, per_device(): lax.ppermute(going_up, 'slab', [(i, (i + 1) % slabs) for i in range(slabs)])  5.3 us
  transfers between devices with their start and end apart: 6, of which 4 were waited for; matrix products, arithmetic and copies ran while one was open for 0% of the time, Pallas kernels for 30%

profile of v5, /device:TPU:0, one launch (start us, length us, event | category | flops | bytes accessed | tf_op | source)
XLA Modules:
  0.0 126.9 jit_solution(17151906164684562446)
XLA Ops:
  0.6 0.0 copy-start.4
  0.6 0.6 copy-done.4
  1.3 0.7 copy.11.route_ref
  2.0 2.0 %shard_map.104 = (f32[8,2176]{1,0:T(8,128)}, f32[8,2176]{1,0:T(8,128)}) custom-call(f32[3,1,4096]{2,1,0:T(1,128)} %bitcast.47, f32[3,1,4096]{2,1,0:T(1,128)} %bitcast.49, s32[2,2048]{1,0:T(2,128)} %bitcast.55, f32[3,1,96]{2,1,0:T(1,128)} %bitcast.56, f32[3,1,96]{2,1,0:T(1,128)} %bitcast.57, s32[1,96]{1,0:T(1,128)} %bitcast.59, s32[96,1]{1,0:T(8,128)} %copy.11.route_ref), custom_call_target="tpu_custom_call" | custom-call | tf_op jit(solution)/shard_map/pallas_call | solution.py:93
  4.1 5.6 %collective-permute-start.1 = (f32[8,2176]{1,0:T(8,128)}, f32[8,2176]{1,0:T(8,128)S(1)}, u32[]{:S(2)}, u32[]{:S(2)}) collective-permute-start(f32[8,2176]{1,0:T(8,128)} %get-tuple-element.20), channel_id=1, source_target_pairs={{8,0},{16,8},{24,16},{32,24},{40,32},{48,40},{56,48},{64,56},{72,6... | collective-permute-start | bytes 208904 | tf_op jit(solution)/shard_map/ppermute | solution.py:448
  9.7 0.0 collective-permute-start
  9.7 0.0 copy-done.3
  9.7 2.2 %collective-permute-done.1.refs_1_ = f32[8,2176]{1,0:T(8,128)S(1)} collective-permute-done((f32[8,2176]{1,0:T(8,128)}, f32[8,2176]{1,0:T(8,128)S(1)}, u32[]{:S(2)}, u32[]{:S(2)}) %collective-permute-start.1) | collective-permute-done | bytes 69664 | tf_op jit(solution)/shard_map/ppermute | solution.py:448
  12.0 5.3 %collective-permute-done.refs_0_ = f32[8,2176]{1,0:T(8,128)S(1)} collective-permute-done((f32[8,2176]{1,0:T(8,128)}, f32[8,2176]{1,0:T(8,128)S(1)}, u32[]{:S(2)}, u32[]{:S(2)}) %collective-permute-start) | collective-permute-done | bytes 69664 | tf_op jit(solution)/shard_map/ppermute | solution.py:447
  17.3 0.1 slice.68
  17.3 0.1 pad_maximum_fusion
  17.4 0.6 broadcast_in_dim.26
  18.1 5.1 %all-to-all-start = ((f32[8,16,128]{2,1,0:T(8,128)}), f32[8,16,128]{2,1,0:T(8,128)S(1)}, u32[]{:S(2)}, u32[]{:S(2)}) async-start(f32[8,16,128]{2,1,0:T(8,128)} %broadcast_in_dim.26), calls=%async_computation | async-start | bytes 131072 | tf_op jit(solution)/shard_map/all_to_all | solution.py:418
  23.1 0.4 shard_map.105
  23.6 1.0 shard_map.106
  24.6 4.8 %all-to-all-done.refs_0_.arrived_ref = f32[8,16,128]{2,1,0:T(8,128)S(1)} async-done(((f32[8,16,128]{2,1,0:T(8,128)}), f32[8,16,128]{2,1,0:T(8,128)S(1)}, u32[]{:S(2)}, u32[]{:S(2)}) %all-to-all-start) | async-done | bytes 65568 | tf_op jit(solution)/shard_map/all_to_all | solution.py:418
  29.4 1.3 %shard_map.109 = (f32[8,8,128]{2,1,0:T(8,128)S(1)}, f32[128,8]{1,0:T(8,128)S(1)}, s32[1,1]{1,0:T(1,128)}) custom-call(f32[8,16,128]{2,1,0:T(8,128)S(1)} %all-to-all-done.refs_0_.arrived_ref), custom_call_target="tpu_custom_call" | custom-call | tf_op jit(solution)/shard_map/pallas_call | solution.py:190
  30.7 15.6 %shard_map.110 = f32[8,8,8,128]{3,2,1,0:T(8,128)} custom-call(s32[1,1]{1,0:T(1,128)} %get-tuple-element.30.refs_0_, f32[8,8,128]{2,1,0:T(8,128)S(1)} %get-tuple-element.31.refs_1_, bf16[32,4096]{1,0:T(8,128)(2,1)S(1)} %get-tuple-element.21.refs_1_.refs_2_.refs_3_, bf16[80,4096]{1,0:T(8,128)(2,1)S(1)} %get-tuple-element.22.refs_2_.refs_3_.refs_4_, ...), custom_call_target="tpu_custom_call" | custom-call | flops 5033164800 | bytes 2457600 | tf_op jit(solution)/shard_map/pallas_call | solution.py:397
  46.3 3.6 %all-to-all-start.2 = ((f32[8,64,128]{2,1,0:T(8,128)}), f32[8,64,128]{2,1,0:T(8,128)S(1)}, u32[]{:S(2)}, u32[]{:S(2)}) async-start(f32[8,64,128]{2,1,0:T(8,128)} %bitcast.13), calls=%async_computation.2 | async-start | bytes 524288 | tf_op jit(solution)/shard_map/all_to_all | solution.py:418
  49.9 21.3 %shard_map.107 = f32[8,8,8,128]{3,2,1,0:T(8,128)} custom-call(f32[8,16,128]{2,1,0:T(8,128)S(1)} %all-to-all-done.refs_0_.arrived_ref, bf16[32,4096]{1,0:T(8,128)(2,1)S(1)} %get-tuple-element.21.refs_1_.refs_2_.refs_3_, bf16[80,4096]{1,0:T(8,128)(2,1)S(1)} %get-tuple-element.22.refs_2_.refs_3_.refs_4_, ...), custom_call_target="tpu_custom_call" | custom-call | flops 5033164800 | bytes 2457600 | tf_op jit(solution)/shard_map/pallas_call | solution.py:397
  71.2 0.1 copy.12
  71.2 0.1 reshape.34.rank_ref
  71.3 0.0 all-to-all-done.2
  71.4 5.4 %all-to-all-start.1 = ((f32[8,64,128]{2,1,0:T(8,128)}), f32[8,64,128]{2,1,0:T(8,128)S(1)}, u32[]{:S(2)}, u32[]{:S(2)}) async-start(f32[8,64,128]{2,1,0:T(8,128)} %bitcast.7), calls=%async_computation.1 | async-start | bytes 524288 | tf_op jit(solution)/shard_map/all_to_all | solution.py:418
  76.8 15.0 %shard_map.111 = (f32[1,8,8,128]{3,2,1,0:T(8,128)S(1)}, f32[8,8,128]{2,1,0:T(8,128)S(1)}) custom-call(s32[1,1]{1,0:T(1,128)} %get-tuple-element.30.refs_0_, f32[8,8,128]{2,1,0:T(8,128)S(1)} %get-tuple-element.31.refs_1_, f32[8,8,8,128]{3,2,1,0:T(8,128)S(1)} %bitcast.45, bf16[32,4096]{1,0:T(8,128)(2,1)S(1)} %get-tuple-element.21.refs_1_.refs_2_.refs_3_, ...), custom_call_target="tpu_custom_call" | custom-call | flops 5033164800 | bytes 2457600 | tf_op jit(solution)/shard_map/pallas_call | solution.py:397
  91.7 0.0 all-to-all-done.1
  91.8 20.9 %shard_map.108 = (f32[1,8,8,128]{3,2,1,0:T(8,128)S(1)}, f32[8,8,128]{2,1,0:T(8,128)S(1)}) custom-call(f32[8,16,128]{2,1,0:T(8,128)S(1)} %all-to-all-done.refs_0_.arrived_ref, f32[8,8,8,128]{3,2,1,0:T(8,128)S(1)} %bitcast.46, bf16[32,4096]{1,0:T(8,128)(2,1)S(1)} %get-tuple-element.21.refs_1_.refs_2_.refs_3_, ...), custom_call_target="tpu_custom_call" | custom-call | flops 5033164800 | bytes 2457600 | tf_op jit(solution)/shard_map/pallas_call | solution.py:397
  112.6 1.1 shard_map.112
  113.7 5.7 %all-to-all-start.3 = ((f32[8,16,128]{2,1,0:T(8,128)}), f32[8,16,128]{2,1,0:T(8,128)S(1)}, u32[]{:S(2)}, u32[]{:S(2)}) async-start(f32[8,16,128]{2,1,0:T(8,128)} %get-tuple-element.34), calls=%async_computation.3 | async-start | bytes 131072 | tf_op jit(solution)/shard_map/all_to_all | solution.py:418
  119.4 6.2 %all-to-all-done.3 = f32[8,16,128]{2,1,0:T(8,128)S(1)} async-done(((f32[8,16,128]{2,1,0:T(8,128)}), f32[8,16,128]{2,1,0:T(8,128)S(1)}, u32[]{:S(2)}, u32[]{:S(2)}) %all-to-all-start.3) | async-done | bytes 65568 | tf_op jit(solution)/shard_map/all_to_all | solution.py:418
  125.7 0.6 copy.13
  126.3 0.6 copy.14
  (20 shorter events, 0.1 us)
Async XLA Ops:
  0.6 0.7 copy-start.4
  4.1 5.7 %copy-start.2 = (f32[1,1,3,128]{3,1,2,0:T(1,128)S(1)}, f32[1,1,3,128]{3,1,2,0:T(1,128)}, u32[]{:S(2)}) copy-start(f32[1,1,3,128]{3,1,2,0:T(1,128)} %param.13) | copy-start | bytes 4612
  4.1 5.7 %copy-start.3 = (f32[1,1,3,128]{3,1,2,0:T(1,128)S(1)}, f32[1,1,3,128]{3,1,2,0:T(1,128)}, u32[]{:S(2)}) copy-start(f32[1,1,3,128]{3,1,2,0:T(1,128)} %param.12) | copy-start | bytes 4612
  4.1 7.9 %collective-permute-start.1 = (f32[8,2176]{1,0:T(8,128)}, f32[8,2176]{1,0:T(8,128)S(1)}, u32[]{:S(2)}, u32[]{:S(2)}) collective-permute-start(f32[8,2176]{1,0:T(8,128)} %get-tuple-element.20), channel_id=1, source_target_pairs={{8,0},{16,8},{24,16},{32,24},{40,32},{48,40},{56,48},{64,56},{72,6... | collective-permute-start | bytes 208904 | tf_op jit(solution)/shard_map/ppermute | solution.py:448
  9.7 7.6 %collective-permute-start = (f32[8,2176]{1,0:T(8,128)}, f32[8,2176]{1,0:T(8,128)S(1)}, u32[]{:S(2)}, u32[]{:S(2)}) collective-permute-start(f32[8,2176]{1,0:T(8,128)} %get-tuple-element.19), channel_id=1, source_target_pairs={{0,8},{8,16},{16,24},{24,32},{32,40},{40,48},{48,56},{56,64},{64,7... | collective-permute-start | bytes 208904 | tf_op jit(solution)/shard_map/ppermute | solution.py:447
  18.1 5.1 %copy-start = (f32[1,1,3,4096]{3,1,2,0:T(1,128)S(1)}, f32[1,1,3,4096]{3,1,2,0:T(1,128)}, u32[]{:S(2)}) copy-start(f32[1,1,3,4096]{3,1,2,0:T(1,128)} %param.9) | copy-start | bytes 147460
  18.1 5.1 %copy-start.1 = (f32[1,1,3,4096]{3,1,2,0:T(1,128)S(1)}, f32[1,1,3,4096]{3,1,2,0:T(1,128)}, u32[]{:S(2)}) copy-start(f32[1,1,3,4096]{3,1,2,0:T(1,128)} %param.10) | copy-start | bytes 147460
  18.1 11.3 %all-to-all-start = ((f32[8,16,128]{2,1,0:T(8,128)}), f32[8,16,128]{2,1,0:T(8,128)S(1)}, u32[]{:S(2)}, u32[]{:S(2)}) async-start(f32[8,16,128]{2,1,0:T(8,128)} %broadcast_in_dim.26), calls=%async_computation | async-start | bytes 131072 | tf_op jit(solution)/shard_map/all_to_all | solution.py:418
  46.3 25.0 %all-to-all-start.2 = ((f32[8,64,128]{2,1,0:T(8,128)}), f32[8,64,128]{2,1,0:T(8,128)S(1)}, u32[]{:S(2)}, u32[]{:S(2)}) async-start(f32[8,64,128]{2,1,0:T(8,128)} %bitcast.13), calls=%async_computation.2 | async-start | bytes 524288 | tf_op jit(solution)/shard_map/all_to_all | solution.py:418
  71.4 20.4 %all-to-all-start.1 = ((f32[8,64,128]{2,1,0:T(8,128)}), f32[8,64,128]{2,1,0:T(8,128)S(1)}, u32[]{:S(2)}, u32[]{:S(2)}) async-start(f32[8,64,128]{2,1,0:T(8,128)} %bitcast.7), calls=%async_computation.1 | async-start | bytes 524288 | tf_op jit(solution)/shard_map/all_to_all | solution.py:418
  113.7 12.0 %all-to-all-start.3 = ((f32[8,16,128]{2,1,0:T(8,128)}), f32[8,16,128]{2,1,0:T(8,128)S(1)}, u32[]{:S(2)}, u32[]{:S(2)}) async-start(f32[8,16,128]{2,1,0:T(8,128)} %get-tuple-element.34), calls=%async_computation.3 | async-start | bytes 131072 | tf_op jit(solution)/shard_map/all_to_all | solution.py:418

commit v6 on v3

--- a/solution.py
+++ b/solution.py
@@ -204,12 +204,10 @@
         jnp.concatenate([ref[m] for m in range(groups)], axis=1) for ref in (moved_ref, table_ref)
     ]
     pieces = jnp.concatenate(three_pieces(jnp.concatenate(rows, axis=0)), axis=0).astype(bf16)
-    wanted = lax.broadcasted_iota(jnp.int32, (slots, groups * slots), 1).astype(f32)
+    wanted = lax.broadcasted_iota(jnp.int32, (groups * slots, slots), 0).astype(f32)
     for member in range(groups):
-        chosen = jnp.where(rank_ref[:, member : member + 1] == wanted, 1.0, 0.0).astype(bf16)
-        found = lax.dot_general(
-            pieces, chosen, (((1,), (1,)), ((), ())), preferred_element_type=f32
-        )
+        chosen = jnp.where(rank_ref[member : member + 1, :] == wanted, 1.0, 0.0).astype(bf16)
+        found = dot(pieces, chosen)
         found = found[0:16] + found[16:32] + found[32:48]
         sums_ref[member, 0:8, :] = own_ref[member]
         sums_ref[member, 8:16, :] = found[0:8]
@@ -456,7 +454,7 @@
     moved_b = swap(first_b.reshape(groups, -1, 128)).reshape(first_b.shape)
     second_a, table_a = pair_sums(received, sets, 1, moved=moved_a)
     second_b, table_b = pair_sums(table_b, sets, 1, moved=moved_b, count=count)
-    rank = rank.reshape(2, groups, CAP, groups).transpose(0, 3, 2, 1).reshape(rank.shape)
+    rank = rank.reshape(2, groups, CAP, groups).transpose(1, 0, 3, 2).reshape(groups, 2 * slots)
     sums, table_b = expand_slots(rank, second_a[0], second_b[0], table_b)
     sums = swap(sums)
     member = lax.axis_index("grp")

time: 125 us -> 127 us (1.016)
  Pallas kernels: 75.6 us -> 76.9 us
    pallas_call x4, Pallas kernels: 71 us -> 72.7 us  [pair_sums(): pl.pallas_call(functools.partial(pairs_kernel, len(source_sets), moved is...]
where the time goes in v6:
time: 127 us; the launch traced here: 126 us
  Pallas kernels  76.9 us (61%)
  starting transfers between devices  25.3 us (20%)
  waiting for transfers between devices  18.4 us (14%)
  local copies, waits for them, and re-layouts  4.51 us (4%)
    pallas_call x4, Pallas kernels, pair_sums(): pl.pallas_call(functools.partial(pairs_kernel, len(source_sets), moved is...  72.7 us
    all_to_all x4, starting transfers between devices, swap(): lax.all_to_all(values, 'grp', split_axis=0, concat_axis=0, tiled=True)  19.6 us
    all_to_all x4, waiting for transfers between devices, swap(): lax.all_to_all(values, 'grp', split_axis=0, concat_axis=0, tiled=True)  11.1 us
    ppermute x1, starting transfers between devices, per_device(): lax.ppermute(going_down, 'slab', [((i + 1) % slabs, i) for i in range(sla...  5.64 us
    ppermute x1, waiting for transfers between devices, per_device(): lax.ppermute(going_up, 'slab', [(i, (i + 1) % slabs) for i in range(slabs)])  5.4 us
    unnamed x21, local copies, waits for them, and re-layouts  3.47 us
  transfers between devices with their start and end apart: 6, of which 4 were waited for; matrix products, arithmetic and copies ran while one was open for 0% of the time, Pallas kernels for 30%

profile of v6, /device:TPU:0, one launch (start us, length us, event | category | flops | bytes accessed | tf_op | source)
XLA Modules:
  0.0 126.0 jit_solution(15125789563228582815)
XLA Ops:
  0.6 0.6 copy-done.7
  1.3 0.1 copy.11.route_ref
  1.4 0.1 copy-done.2
  1.4 0.9 copy_bitcast_fusion
  2.4 0.0 copy-start
  2.4 0.0 copy-start.1
  2.4 0.7 copy-done
  3.1 0.5 shard_map.104
  3.6 5.6 %collective-permute-start.1 = (f32[8,2176]{1,0:T(8,128)S(1)}, f32[8,2176]{1,0:T(8,128)S(1)}, u32[]{:S(2)}, u32[]{:S(2)}) collective-permute-start(f32[8,2176]{1,0:T(8,128)S(1)} %get-tuple-element.20), channel_id=1, source_target_pairs={{8,0},{16,8},{24,16},{32,24},{40,32},{48,40},{56,48},{64,56},{72,6... | collective-permute-start | bytes 208904 | tf_op jit(solution)/shard_map/ppermute | solution.py:442
  9.2 1.9 %collective-permute-done.1.refs_1_ = f32[8,2176]{1,0:T(8,128)S(1)} collective-permute-done((f32[8,2176]{1,0:T(8,128)S(1)}, f32[8,2176]{1,0:T(8,128)S(1)}, u32[]{:S(2)}, u32[]{:S(2)}) %collective-permute-start.1) | collective-permute-done | bytes 69664 | tf_op jit(solution)/shard_map/ppermute | solution.py:442
  11.2 5.4 %collective-permute-done.refs_0_ = f32[8,2176]{1,0:T(8,128)S(1)} collective-permute-done((f32[8,2176]{1,0:T(8,128)S(1)}, f32[8,2176]{1,0:T(8,128)S(1)}, u32[]{:S(2)}, u32[]{:S(2)}) %collective-permute-start) | collective-permute-done | bytes 69664 | tf_op jit(solution)/shard_map/ppermute | solution.py:441
  16.6 0.1 slice.68
  16.6 0.1 pad_maximum_fusion
  16.7 0.6 broadcast_in_dim.20
  17.4 4.9 %all-to-all-start = ((f32[8,16,128]{2,1,0:T(8,128)}), f32[8,16,128]{2,1,0:T(8,128)S(1)}, u32[]{:S(2)}, u32[]{:S(2)}) async-start(f32[8,16,128]{2,1,0:T(8,128)} %broadcast_in_dim.20), calls=%async_computation | async-start | bytes 131072 | tf_op jit(solution)/shard_map/all_to_all | solution.py:416
  22.3 0.4 shard_map.105
  22.8 1.0 shard_map.106
  23.7 4.8 %all-to-all-done.refs_0_.arrived_ref = f32[8,16,128]{2,1,0:T(8,128)S(1)} async-done(((f32[8,16,128]{2,1,0:T(8,128)}), f32[8,16,128]{2,1,0:T(8,128)S(1)}, u32[]{:S(2)}, u32[]{:S(2)}) %all-to-all-start) | async-done | bytes 65568 | tf_op jit(solution)/shard_map/all_to_all | solution.py:416
  28.6 1.3 %shard_map.109 = (f32[8,8,128]{2,1,0:T(8,128)S(1)}, f32[128,8]{1,0:T(8,128)S(1)}, s32[1,1]{1,0:T(1,128)}) custom-call(f32[8,16,128]{2,1,0:T(8,128)S(1)} %all-to-all-done.refs_0_.arrived_ref), custom_call_target="tpu_custom_call" | custom-call | tf_op jit(solution)/shard_map/pallas_call | solution.py:188
  29.8 15.6 %shard_map.110 = f32[8,8,8,128]{3,2,1,0:T(8,128)} custom-call(s32[1,1]{1,0:T(1,128)} %get-tuple-element.30.refs_0_, f32[8,8,128]{2,1,0:T(8,128)S(1)} %get-tuple-element.31.refs_1_, bf16[32,4096]{1,0:T(8,128)(2,1)S(1)} %get-tuple-element.21.refs_1_.refs_2_.refs_3_, bf16[80,4096]{1,0:T(8,128)(2,1)S(1)} %get-tuple-element.22.refs_2_.refs_3_.refs_4_, ...), custom_call_target="tpu_custom_call" | custom-call | flops 5033164800 | bytes 2457600 | tf_op jit(solution)/shard_map/pallas_call | solution.py:395
  45.5 3.6 %all-to-all-start.2 = ((f32[8,64,128]{2,1,0:T(8,128)}), f32[8,64,128]{2,1,0:T(8,128)S(1)}, u32[]{:S(2)}, u32[]{:S(2)}) async-start(f32[8,64,128]{2,1,0:T(8,128)} %bitcast.9), calls=%async_computation.2 | async-start | bytes 524288 | tf_op jit(solution)/shard_map/all_to_all | solution.py:416
  49.1 21.3 %shard_map.107 = f32[8,8,8,128]{3,2,1,0:T(8,128)} custom-call(f32[8,16,128]{2,1,0:T(8,128)S(1)} %all-to-all-done.refs_0_.arrived_ref, bf16[32,4096]{1,0:T(8,128)(2,1)S(1)} %get-tuple-element.21.refs_1_.refs_2_.refs_3_, bf16[80,4096]{1,0:T(8,128)(2,1)S(1)} %get-tuple-element.22.refs_2_.refs_3_.refs_4_, ...), custom_call_target="tpu_custom_call" | custom-call | flops 5033164800 | bytes 2457600 | tf_op jit(solution)/shard_map/pallas_call | solution.py:395
  70.3 0.1 copy.12
  70.4 0.1 reshape.34.rank_ref
  70.5 5.4 %all-to-all-start.1 = ((f32[8,64,128]{2,1,0:T(8,128)}), f32[8,64,128]{2,1,0:T(8,128)S(1)}, u32[]{:S(2)}, u32[]{:S(2)}) async-start(f32[8,64,128]{2,1,0:T(8,128)} %bitcast.3), calls=%async_computation.1 | async-start | bytes 524288 | tf_op jit(solution)/shard_map/all_to_all | solution.py:416
  75.9 15.0 %shard_map.111 = (f32[1,8,8,128]{3,2,1,0:T(8,128)S(1)}, f32[8,8,128]{2,1,0:T(8,128)S(1)}) custom-call(s32[1,1]{1,0:T(1,128)} %get-tuple-element.30.refs_0_, f32[8,8,128]{2,1,0:T(8,128)S(1)} %get-tuple-element.31.refs_1_, f32[8,8,8,128]{3,2,1,0:T(8,128)S(1)} %bitcast.41, bf16[32,4096]{1,0:T(8,128)(2,1)S(1)} %get-tuple-element.21.refs_1_.refs_2_.refs_3_, ...), custom_call_target="tpu_custom_call" | custom-call | flops 5033164800 | bytes 2457600 | tf_op jit(solution)/shard_map/pallas_call | solution.py:395
  90.9 20.9 %shard_map.108 = (f32[1,8,8,128]{3,2,1,0:T(8,128)S(1)}, f32[8,8,128]{2,1,0:T(8,128)S(1)}) custom-call(f32[8,16,128]{2,1,0:T(8,128)S(1)} %all-to-all-done.refs_0_.arrived_ref, f32[8,8,8,128]{3,2,1,0:T(8,128)S(1)} %bitcast.42, bf16[32,4096]{1,0:T(8,128)(2,1)S(1)} %get-tuple-element.21.refs_1_.refs_2_.refs_3_, ...), custom_call_target="tpu_custom_call" | custom-call | flops 5033164800 | bytes 2457600 | tf_op jit(solution)/shard_map/pallas_call | solution.py:395
  111.8 1.1 shard_map.112
  112.9 5.7 %all-to-all-start.3 = ((f32[8,16,128]{2,1,0:T(8,128)}), f32[8,16,128]{2,1,0:T(8,128)S(1)}, u32[]{:S(2)}, u32[]{:S(2)}) async-start(f32[8,16,128]{2,1,0:T(8,128)} %get-tuple-element.34), calls=%async_computation.3 | async-start | bytes 131072 | tf_op jit(solution)/shard_map/all_to_all | solution.py:416
  118.6 6.2 %all-to-all-done.3 = f32[8,16,128]{2,1,0:T(8,128)S(1)} async-done(((f32[8,16,128]{2,1,0:T(8,128)}), f32[8,16,128]{2,1,0:T(8,128)S(1)}, u32[]{:S(2)}, u32[]{:S(2)}) %all-to-all-start.3) | async-done | bytes 65568 | tf_op jit(solution)/shard_map/all_to_all | solution.py:416
  124.9 0.6 copy.13
  125.5 0.6 copy.14
  (28 shorter events, 0.1 us)
Async XLA Ops:
  0.6 0.7 copy-start.7
  0.6 0.8 copy-start.2
  1.4 0.9 copy-start.3
  1.4 0.9 copy-start.4
  2.4 0.7 copy-start
  2.4 0.7 copy-start.1
  3.6 5.7 %copy-start.5 = (f32[1,1,3,128]{3,1,2,0:T(1,128)S(1)}, f32[1,1,3,128]{3,1,2,0:T(1,128)}, u32[]{:S(2)}) copy-start(f32[1,1,3,128]{3,1,2,0:T(1,128)} %param.13) | copy-start | bytes 4612
  3.6 5.7 %copy-start.6 = (f32[1,1,3,128]{3,1,2,0:T(1,128)S(1)}, f32[1,1,3,128]{3,1,2,0:T(1,128)}, u32[]{:S(2)}) copy-start(f32[1,1,3,128]{3,1,2,0:T(1,128)} %param.12) | copy-start | bytes 4612
  3.6 7.6 %collective-permute-start.1 = (f32[8,2176]{1,0:T(8,128)S(1)}, f32[8,2176]{1,0:T(8,128)S(1)}, u32[]{:S(2)}, u32[]{:S(2)}) collective-permute-start(f32[8,2176]{1,0:T(8,128)S(1)} %get-tuple-element.20), channel_id=1, source_target_pairs={{8,0},{16,8},{24,16},{32,24},{40,32},{48,40},{56,48},{64,56},{72,6... | collective-permute-start | bytes 208904 | tf_op jit(solution)/shard_map/ppermute | solution.py:442
  9.2 7.3 %collective-permute-start = (f32[8,2176]{1,0:T(8,128)S(1)}, f32[8,2176]{1,0:T(8,128)S(1)}, u32[]{:S(2)}, u32[]{:S(2)}) collective-permute-start(f32[8,2176]{1,0:T(8,128)S(1)} %get-tuple-element.19), channel_id=1, source_target_pairs={{0,8},{8,16},{16,24},{24,32},{32,40},{40,48},{48,56},{56,64},{64,7... | collective-permute-start | bytes 208904 | tf_op jit(solution)/shard_map/ppermute | solution.py:441
  17.4 11.2 %all-to-all-start = ((f32[8,16,128]{2,1,0:T(8,128)}), f32[8,16,128]{2,1,0:T(8,128)S(1)}, u32[]{:S(2)}, u32[]{:S(2)}) async-start(f32[8,16,128]{2,1,0:T(8,128)} %broadcast_in_dim.20), calls=%async_computation | async-start | bytes 131072 | tf_op jit(solution)/shard_map/all_to_all | solution.py:416
  45.5 25.1 %all-to-all-start.2 = ((f32[8,64,128]{2,1,0:T(8,128)}), f32[8,64,128]{2,1,0:T(8,128)S(1)}, u32[]{:S(2)}, u32[]{:S(2)}) async-start(f32[8,64,128]{2,1,0:T(8,128)} %bitcast.9), calls=%async_computation.2 | async-start | bytes 524288 | tf_op jit(solution)/shard_map/all_to_all | solution.py:416
  70.5 20.4 %all-to-all-start.1 = ((f32[8,64,128]{2,1,0:T(8,128)}), f32[8,64,128]{2,1,0:T(8,128)S(1)}, u32[]{:S(2)}, u32[]{:S(2)}) async-start(f32[8,64,128]{2,1,0:T(8,128)} %bitcast.3), calls=%async_computation.1 | async-start | bytes 524288 | tf_op jit(solution)/shard_map/all_to_all | solution.py:416
  112.9 12.0 %all-to-all-start.3 = ((f32[8,16,128]{2,1,0:T(8,128)}), f32[8,16,128]{2,1,0:T(8,128)S(1)}, u32[]{:S(2)}, u32[]{:S(2)}) async-start(f32[8,16,128]{2,1,0:T(8,128)} %get-tuple-element.34), calls=%async_computation.3 | async-start | bytes 131072 | tf_op jit(solution)/shard_map/all_to_all | solution.py:416
